TPU v7x, 32 devices: a whole 2x2x4 slice. The times are simulated.
32 devices in a mesh: groups: 2 (over x), pool: 16 (over z, y, core).
Axes of the slice: x: 2, y: 2, z: 4, core: 2. Of those that a mesh axis runs over, the one named last changes fastest.
Arguments:
- normed_input_rows: bfloat16 [256, 8192], P(('groups', 'pool')), parts along dimension 0, may hold values from -6 to 6
- gate_base_weight: bfloat16 [8192, 28672], P(None, 'pool'), may hold values from -0.0625 to 0.0625
- adapter_down_factors: bfloat16 [32, 64, 8192], P(('groups', 'pool')), parts along dimension 0, may hold values from -0.0625 to 0.0625
- adapter_up_factors: bfloat16 [32, 64, 28672], P(('groups', 'pool')), parts along dimension 0, may hold values from -0.75 to 0.75
- request_adapter_id: int32 [64, 1], P('groups'), parts along dimension 0, may hold values from 0 to 15; in each aligned block of 32 rows (0 to 31, 32 to 63, ...) at most 3 rows name the same one
- row_request: int32 [256], P('groups'), parts along dimension 0, may hold values from 0 to 31, never falling along the last dimension, each value on 1 to 8 neighbouring positions
- adapter_storage_slot: int32 [32], P('groups'), parts along dimension 0, may hold values from 0 to 15, each once
Outputs:
- gate_out: bfloat16 [256, 28672], P('groups', 'pool'), parts along dimension 0
There are 2 independent parts, one for each index of `groups`. A program takes and returns all parts, laid end to end along the dimension named above; an argument that names none is the same for every part. Nothing has to cross between parts.
Inputs may be any that keep to these rules, and one draw needn't show every extreme that they name: `request_adapter_id`: every adapter serves at least one request and at most 3 requests; some adapter serves exactly 3. `row_request`: rows of one request are consecutive, requests in increasing order, each of 1 to 8 rows. `adapter_storage_slot`: a permutation: each slot holds exactly one adapter; slot s lies on pool index s.
All inputs are finite; a program needn't handle non-finite values.
Results may differ from a plain program's by a relative error of at most 0.004.
Values may be sent and summed in bfloat16 or wider, within the bound.
No kernel may reach another device: no remote copies, remote signals or barrier semaphores. Data moves between devices by JAX's collectives and lax.ppermute only.
A program may use at most 192 MiB of HBM per device.

v0:
```python
import jax
import jax.numpy as jnp
from jax import lax
from jax.sharding import PartitionSpec as P

ROW_CAP = 24


def on_device(
    normed_input_rows,
    gate_base_weight,
    adapter_down_factors,
    adapter_up_factors,
    request_adapter_id,
    row_request,
    adapter_storage_slot,
):
    member = lax.axis_index("pool")
    npool = lax.axis_size("pool")
    local_share = adapter_down_factors.shape[0]
    width = gate_base_weight.shape[1]
    row_slot = jnp.take(adapter_storage_slot, jnp.take(request_adapter_id[:, 0], row_request))
    shard_piece = lax.all_gather(normed_input_rows, "pool", axis=0, tiled=True)
    every_adapter = jnp.einsum(
        "aw,qtw->aqt", shard_piece, adapter_down_factors, preferred_element_type=jnp.float32
    )
    owned = (
        row_slot[:, None]
        == member * local_share + jnp.arange(local_share, dtype=jnp.int32)[None, :]
    ).astype(jnp.float32)
    lowpart = jnp.sum(every_adapter * owned[:, :, None], axis=1)
    basepart = jnp.dot(shard_piece, gate_base_weight, preferred_element_type=jnp.float32)
    joined = jnp.concatenate([basepart, lowpart], axis=1)
    base = joined[:, :width]
    low = lax.psum(joined[:, width:], "pool").astype(jnp.bfloat16)
    total_rows = base.shape[0]
    rank_width = low.shape[1]
    owner = row_slot // local_share
    owner_hot = (owner[:, None] == jnp.arange(npool, dtype=jnp.int32)[None, :]).astype(jnp.int32)
    earlier = jnp.cumsum(owner_hot, axis=0) - owner_hot
    position = jnp.sum(earlier * owner_hot, axis=1)
    mine = owner == member
    select = (
        (position[None, :] == jnp.arange(ROW_CAP, dtype=jnp.int32)[:, None]) & mine[None, :]
    ).astype(jnp.bfloat16)
    which = row_slot - member * local_share
    which_hot = (which[:, None] == jnp.arange(local_share, dtype=jnp.int32)[None, :]).astype(
        jnp.bfloat16
    )
    weighted = (which_hot[:, :, None] * low[:, None, :]).reshape(
        total_rows, local_share * rank_width
    )
    chosen = jnp.dot(select, weighted, preferred_element_type=jnp.float32).astype(jnp.bfloat16)
    results = jnp.dot(
        chosen,
        adapter_up_factors.reshape(local_share * rank_width, adapter_up_factors.shape[2]),
        preferred_element_type=jnp.float32,
    )
    received = lax.all_to_all(results, "pool", split_axis=1, concat_axis=0, tiled=True)
    delta = jnp.take(received, owner * ROW_CAP + position, axis=0)
    return (base + delta).astype(jnp.bfloat16)


def solution(mesh):
    in_specs = (
        P(("groups", "pool"), None),
        P(None, "pool"),
        P(("groups", "pool"), None, None),
        P(("groups", "pool"), None, None),
        P("groups", None),
        P("groups"),
        P("groups"),
    )
    out_specs = P("groups", "pool")
    return jax.shard_map(
        on_device, mesh=mesh, in_specs=in_specs, out_specs=out_specs, check_vma=False
    )
```

profile of v0, /device:TPU:13, one launch (start us, length us, event | category | flops | bytes accessed | tf_op | source)
XLA Modules:
  0.0 208.7 jit_solution(2206446665557751418)
XLA Ops:
  6.5 0.0 copy-start
  6.5 0.0 all-gather.2.cloned.1.call-start
  6.5 0.7 all-gather.2.cloned.1.call-update
  7.3 0.7 compare_select_fusion.2
  7.9 1.6 gather_fusion
  9.5 2.0 fusion.21
  11.5 10.6 %compare_convert_fusion = (bf16[128]{0:T(256)(128)(2,1)S(1)}, s32[128]{0:T(128)S(1)}) fusion(s32[]{:T(128)S(6)} %axis_index.12, s32[]{:T(128)} %bitcast.16, s32[]{:T(128)} %bitcast.15, s32[]{:T(128)} %bitcast.14, s32[]{:T(128)} %bitcast.13, s32[]{:T(128)} %bitcast.12, s32[]{:T(128)} %bitcast.11, s32[]{:T(128)} %bitcast.10, s32[]{:T(128)} %bitcast.9, ...), kind=kLoop, calls=%fused_computation.41 | loop fusion | flops 6016 | bytes 1860 | tf_op jit(solution)/shard_map/convert_element_type | solution.py:47
  22.1 0.1 fusion.6
  22.2 0.2 reduce_window_sum.11
  22.4 0.2 select_reduce_fusion
  22.5 28.1 %all-gather.2.cloned.1.call-done = bf16[128,8192]{1,0:T(8,128)(2,1)} async-done(((bf16[8,8192]{1,0:T(8,128)(2,1)}), bf16[128,8192]{1,0:T(8,128)(2,1)}) %all-gather.2.cloned.1.call-update) | async-done | bytes 2097168 | tf_op jit(solution)/shard_map/all_gather | solution.py:23
  50.6 0.0 copy-done
  50.6 2.3 %convolution_multiply_fusion = f32[128,64]{1,0:T(8,128)S(1)} fusion(bf16[128,8192]{1,0:T(8,128)(2,1)} %all-gather.2.cloned.1.call-done, bf16[1,64,8192]{2,1,0:T(8,128)(2,1)S(1)} %copy-done, f32[128]{0:T(128)S(1)} %get-tuple-element.11), kind=kOutput, calls=%fused_computation.7 | convolution fusion | flops 134225920 | bytes 3179008 | tf_op jit(solution)/shard_map/aw,qtw->aqt/dot_general | solution.py:24
  52.9 44.9 %psum.7 = bf16[128,64]{1,0:T(8,128)(2,1)S(1)} all-reduce(f32[128,64]{1,0:T(8,128)S(1)} %convolution_multiply_fusion), channel_id=1, replica_groups=mesh['groups'=2,'pool'=16] {'pool'}, use_global_device_ids=true, to_apply=%region_2.3 | all-reduce | flops 8192 | bytes 49152 | tf_op jit(solution)/shard_map/psum | solution.py:35
  97.8 4.4 %fusion = f32[24,16,1792]{2,0,1:T(8,128)} fusion(bf16[8,16,8,1792]{3,2,1,0:T(8,128)(2,1)} %bitcast.38, bf16[128,64]{1,0:T(8,128)(2,1)S(1)} %psum.7, bf16[128]{0:T(256)(128)(2,1)S(1)} %get-tuple-element.7, s32[128]{0:T(128)S(1)} %select_reduce_fusion, pred[128]{0:T(512)(128)(4,1)S(1)} %get-tuple-element.12), kind=kOutput, calls=%fused_computation.2 | convolution fusion | flops 88489472 | bytes 6439808 | tf_op jit(solution)/shard_map/dot_general | solution.py:54
  102.2 21.1 %all-to-all-start = ((f32[24,16,1792]{2,0,1:T(8,128)}), f32[24,16,1792]{2,0,1:T(8,128)}, u32[]{:S(2)}, u32[]{:S(2)}) async-start(f32[24,16,1792]{2,0,1:T(8,128)} %fusion), calls=%async_computation | async-start | bytes 5505024 | tf_op jit(solution)/shard_map/all_to_all | solution.py:59
  123.4 61.6 %all-to-all-done = f32[24,16,1792]{2,0,1:T(8,128)} async-done(((f32[24,16,1792]{2,0,1:T(8,128)}), f32[24,16,1792]{2,0,1:T(8,128)}, u32[]{:S(2)}, u32[]{:S(2)}) %all-to-all-start) | async-done | bytes 2752544 | tf_op jit(solution)/shard_map/all_to_all | solution.py:59
  185.0 0.0 copy-start.1
  185.0 4.2 %gather_fusion.1 = f32[128,1792]{1,0:T(8,128)} fusion(f32[384,1792]{1,0:T(8,128)} %bitcast.22, s32[1024]{0:T(1024)S(1)} %pad_clamp_fusion), kind=kCustom, calls=%fused_computation.1 | custom fusion | bytes 1835520 | tf_op jit(solution)/shard_map/jit(_take)/gather | solution.py:60
  189.1 0.0 copy-done.1
  189.1 12.7 %fusion.3 = bf16[128,1792]{1,0:T(8,128)(2,1)} fusion(bf16[128,8192]{1,0:T(8,128)(2,1)S(1)} %copy-done.1, bf16[8192,1792]{1,0:T(8,128)(2,1)} %param.8, f32[128,1792]{1,0:T(8,128)} %gather_fusion.1, pred[128]{0:T(512)(128)(4,1)S(1)} %get-tuple-element.5), kind=kOutput, calls=%fused_computation.6 | convolution fusion | flops 3758784512 | bytes 32833664 | tf_op jit(solution)/shard_map/dot_general | solution.py:32
  (3 shorter events, 0.0 us)
Async XLA Ops:
  6.5 44.1 %copy-start = (bf16[1,64,8192]{2,1,0:T(8,128)(2,1)S(1)}, bf16[1,64,8192]{2,1,0:T(8,128)(2,1)}, u32[]{:S(2)}) copy-start(bf16[1,64,8192]{2,1,0:T(8,128)(2,1)} %param.9) | copy-start | bytes 3145732
  6.5 44.1 %all-gather.2.cloned.1.call-start = ((), (), s32[]{:S(2)}) async-start(), calls=%async_computation.1 | async-start | bytes 2228224 | tf_op jit(solution)/shard_map/all_gather | solution.py:23
  102.2 82.7 %all-to-all-start = ((f32[24,16,1792]{2,0,1:T(8,128)}), f32[24,16,1792]{2,0,1:T(8,128)}, u32[]{:S(2)}, u32[]{:S(2)}) async-start(f32[24,16,1792]{2,0,1:T(8,128)} %fusion), calls=%async_computation | async-start | bytes 5505024 | tf_op jit(solution)/shard_map/all_to_all | solution.py:59
  185.0 4.2 %copy-start.1 = (bf16[128,8192]{1,0:T(8,128)(2,1)S(1)}, bf16[128,8192]{1,0:T(8,128)(2,1)}, u32[]{:S(2)}) copy-start(bf16[128,8192]{1,0:T(8,128)(2,1)} %all-gather.2.cloned.1.call-done) | copy-start | bytes 6291460
Sparse Core Ops, SparseCore 0:
  9.5 41.0 all-gather.1
where the time goes:
time: 209 us
  waiting for transfers between devices  90.4 us (43%)
  blocking collectives  44.9 us (21%)
  starting transfers between devices  21.1 us (10%)
  matrix products  19.4 us (9%)
  between operations  13.4 us (6%)
  other arithmetic  11.7 us (6%)
  local copies, waits for them, and re-layouts  7.71 us (4%)
    all_to_all x1, waiting for transfers between devices, on_device(): lax.all_to_all(results, 'pool', split_axis=1, concat_axis=0, tiled=True)  61.6 us
    psum x1, blocking collectives, on_device(): low = lax.psum(joined[:, width:], 'pool').astype(jnp.bfloat16)  44.9 us
    all_gather x1, waiting for transfers between devices, on_device(): shard_piece = lax.all_gather(normed_input_rows, 'pool', axis=0, tiled=True)  28.1 us
    all_to_all x1, starting transfers between devices, on_device(): lax.all_to_all(results, 'pool', split_axis=1, concat_axis=0, tiled=True)  21.1 us
    dot_general x1, matrix products, on_device(): jnp.dot(shard_piece, gate_base_weight, preferred_element_type=jnp.float32)  12.7 us
    convert_element_type x1, other arithmetic, on_device(): (which[:, None] == jnp.arange(local_share, dtype=jnp.int32)[None, :]).ast...  10.6 us
    dot_general x1, matrix products, on_device(): jnp.dot(chosen, adapter_up_factors.reshape(local_share * rank_width, adap...  4.4 us
  transfers between devices with their start and end apart: 2, of which 2 were waited for; matrix products, arithmetic and copies ran while one was open for 7% of the time, Pallas kernels for 0%

commit v1 on v0

v1 whole, which is shorter than its diff:
```python
import jax
import jax.numpy as jnp
from jax import lax
from jax.sharding import PartitionSpec as P

ROW_CAP = 24


def on_device(
    normed_input_rows,
    gate_base_weight,
    adapter_down_factors,
    adapter_up_factors,
    request_adapter_id,
    row_request,
    adapter_storage_slot,
):
    member = lax.axis_index("pool")
    npool = lax.axis_size("pool")
    share, rank = adapter_down_factors.shape[:2]
    adapters = npool * share
    requests = request_adapter_id.shape[0]
    request_slot = jnp.sum(
        jnp.where(
            request_adapter_id == jnp.arange(adapters, dtype=jnp.int32)[None, :],
            adapter_storage_slot[None, :],
            0,
        ),
        axis=1,
    )
    row_slot = jnp.sum(
        jnp.where(
            row_request[:, None] == jnp.arange(requests, dtype=jnp.int32)[None, :],
            request_slot[None, :],
            0,
        ),
        axis=1,
    )
    rows = row_slot.shape[0]
    owner = row_slot // share
    before = jnp.arange(rows)[None, :] < jnp.arange(rows)[:, None]
    place = jnp.sum((before & (owner[:, None] == owner[None, :])).astype(jnp.int32), axis=1)

    x = lax.all_gather(normed_input_rows, "pool", axis=0, tiled=True)
    select = (
        (place[None, :] == jnp.arange(ROW_CAP, dtype=jnp.int32)[:, None])
        & (owner == member)[None, :]
    ).astype(jnp.bfloat16)
    low = jnp.dot(
        x,
        adapter_down_factors.reshape(share * rank, -1).T,
        preferred_element_type=jnp.float32,
    ).astype(jnp.bfloat16)
    which = row_slot - member * share
    mine = which[:, None] == jnp.arange(share * rank, dtype=jnp.int32)[None, :] // rank
    low = jnp.where(mine, low, 0)
    chosen = jnp.dot(select, low, preferred_element_type=jnp.float32).astype(jnp.bfloat16)
    terms = jnp.dot(
        chosen,
        adapter_up_factors.reshape(share * rank, -1),
        preferred_element_type=jnp.float32,
    ).astype(jnp.bfloat16)
    received = lax.all_to_all(terms, "pool", split_axis=1, concat_axis=0, tiled=True)
    base = jnp.dot(x, gate_base_weight, preferred_element_type=jnp.float32)
    base, received = lax.optimization_barrier((base, received))
    pick = (
        (owner * ROW_CAP + place)[:, None]
        == jnp.arange(npool * ROW_CAP, dtype=jnp.int32)[None, :]
    ).astype(jnp.bfloat16)
    delta = jnp.dot(pick, received, preferred_element_type=jnp.float32)
    return (base + delta).astype(jnp.bfloat16)


def solution(mesh):
    in_specs = (
        P(("groups", "pool"), None),
        P(None, "pool"),
        P(("groups", "pool"), None, None),
        P(("groups", "pool"), None, None),
        P("groups", None),
        P("groups"),
        P("groups"),
    )
    out_specs = P("groups", "pool")
    return jax.shard_map(
        on_device, mesh=mesh, in_specs=in_specs, out_specs=out_specs, check_vma=False
    )
```

time: 209 us -> 106 us (0.51)
  blocking collectives: 44.9 us -> 0 us
  waiting for transfers between devices: 90.4 us -> 62 us
  starting transfers between devices: 21.1 us -> 6.47 us
  other arithmetic: 11.7 us -> 1.69 us
  local copies, waits for them, and re-layouts: 7.71 us -> 1.19 us
    psum x1 -> x0, blocking collectives: 44.9 us -> none  [on_device(): low = lax.psum(joined[:, width:], 'pool').astype(jnp.bfloat16)]
    all_to_all x1, waiting for transfers between devices: 61.6 us -> 19.7 us  [on_device(): lax.all_to_all(terms, 'pool', split_axis=1, concat_axis=0, tiled=True)]
    all_to_all x1, starting transfers between devices: 21.1 us -> 6.47 us  [on_device(): lax.all_to_all(terms, 'pool', split_axis=1, concat_axis=0, tiled=True)]
    all_gather x1, waiting for transfers between devices: 28.1 us -> 41.6 us  [on_device(): x = lax.all_gather(normed_input_rows, 'pool', axis=0, tiled=True)]
    convert_element_type x2 -> x0, other arithmetic: 10.7 us -> none  [the longest x1 10.6 us: on_device(): (which[:, None] == jnp.arange(local_share, dtype=jnp.int32)[None, :]).ast...]
    gather x3 -> x0, local copies, waits for them, and re-layouts: 7.7 us -> none  [the longest x1 4.16 us: on_device(): delta = jnp.take(received, owner * ROW_CAP + position, axis=0)]
    dot_general x3 -> x4, matrix products: 19.4 us -> 20.4 us  [the longest x1 12.4 us: on_device(): base = jnp.dot(x, gate_base_weight, preferred_element_type=jnp.float32)]
  transfers between devices with their start and end apart: 2 -> 2, of which waited for: 2 -> 2; matrix products, arithmetic and copies ran while one was open for 7% -> 13% of each run, Pallas kernels for 0% -> 0%
where the time goes in v1:
time: 106 us; the launch traced here: 105 us
  waiting for transfers between devices  62 us (58%)
  matrix products  20.4 us (19%)
  between operations  13.4 us (13%)
  starting transfers between devices  6.47 us (6%)
  other arithmetic  1.69 us (2%)
  local copies, waits for them, and re-layouts  1.19 us (1%)
    all_gather x1, waiting for transfers between devices, on_device(): x = lax.all_gather(normed_input_rows, 'pool', axis=0, tiled=True)  41.6 us
    all_to_all x1, waiting for transfers between devices, on_device(): lax.all_to_all(terms, 'pool', split_axis=1, concat_axis=0, tiled=True)  19.7 us
    dot_general x1, matrix products, on_device(): base = jnp.dot(x, gate_base_weight, preferred_element_type=jnp.float32)  12.4 us
    all_to_all x1, starting transfers between devices, on_device(): lax.all_to_all(terms, 'pool', split_axis=1, concat_axis=0, tiled=True)  6.47 us
    dot_general x1, matrix products, on_device(): delta = jnp.dot(pick, received, preferred_element_type=jnp.float32)  2.81 us
    dot_general x1, matrix products, on_device(): jnp.dot(chosen, adapter_up_factors.reshape(share * rank, -1), preferred_e...  2.65 us
    dot_general x1, matrix products, on_device(): jnp.dot(select, low, preferred_element_type=jnp.float32)  2.54 us
  transfers between devices with their start and end apart: 2, of which 2 were waited for; matrix products, arithmetic and copies ran while one was open for 13% of the time, Pallas kernels for 0%

profile of v1, /device:TPU:13, one launch (start us, length us, event | category | flops | bytes accessed | tf_op | source)
XLA Modules:
  0.0 105.2 jit_solution(2164490671110740630)
XLA Ops:
  6.5 0.0 copy-start
  6.5 0.0 all-gather.2.cloned.1.call-start
  6.5 0.7 all-gather.2.cloned.1.call-update
  7.3 0.8 select_reduce_fusion.1
  8.0 0.7 select_reduce_fusion
  8.8 0.2 convert_reduce_fusion
  9.0 41.6 %all-gather.2.cloned.1.call-done = bf16[128,8192]{1,0:T(8,128)(2,1)} async-done(((bf16[8,8192]{1,0:T(8,128)(2,1)}), bf16[128,8192]{1,0:T(8,128)(2,1)}) %all-gather.2.cloned.1.call-update) | async-done | bytes 2097168 | tf_op jit(solution)/shard_map/all_gather | solution.py:44
  50.6 0.0 copy-done
  50.6 2.5 %fusion.4 = bf16[24,64]{1,0:T(8,128)(2,1)S(1)} fusion(bf16[128,8192]{1,0:T(8,128)(2,1)} %all-gather.2.cloned.1.call-done, bf16[1,64,8192]{2,1,0:T(8,128)(2,1)S(1)} %copy-done, s32[128]{0:T(128)S(1)} %get-tuple-element.10, s32[64]{0:T(128)S(1)} %and_select_fusion, s32[128]{0:T(128)S(1)} %convert_reduce_fusion, pred[128]{0:T(512)(128)(4,1)S(1)} %broadcast_compare_fusion), kind=kOutput, calls=%fused_computation.8 | convolution fusion | flops 134643200 | bytes 3150208 | tf_op jit(solution)/shard_map/dot_general | solution.py:57
  53.2 2.6 %convolution_convert_fusion = bf16[24,28672]{1,0:T(8,128)(2,1)S(1)} fusion(bf16[24,64]{1,0:T(8,128)(2,1)S(1)} %fusion.4, bf16[1,64,28672]{2,1,0:T(8,128)(2,1)} %param.10), kind=kOutput, calls=%fused_computation | convolution fusion | flops 88768512 | bytes 5049344 | tf_op jit(solution)/shard_map/dot_general | solution.py:58
  55.8 0.0 copy-start.1
  55.8 1.2 %copy.12 = bf16[3,16,8,1792]{3,2,0,1:T(8,128)(2,1)} copy(bf16[3,16,8,1792]{3,2,1,0:T(8,128)(2,1)S(1)} %bitcast.21) | data formatting | bytes 2752512 | tf_op jit(solution)/shard_map/all_to_all | solution.py:63
  57.0 6.5 %all-to-all-start = ((bf16[24,16,1792]{2,0,1:T(8,128)(2,1)}), bf16[24,16,1792]{2,0,1:T(8,128)(2,1)}, u32[]{:S(2)}, u32[]{:S(2)}) async-start(bf16[24,16,1792]{2,0,1:T(8,128)(2,1)} %bitcast.20), calls=%async_computation | async-start | bytes 2752512 | tf_op jit(solution)/shard_map/all_to_all | solution.py:63
  63.5 0.0 copy-done.1
  63.5 12.4 %fusion.18 = f32[128,1792]{1,0:T(8,128)} fusion(bf16[128,8192]{1,0:T(8,128)(2,1)S(1)} %copy-done.1, bf16[8192,1792]{1,0:T(8,128)(2,1)} %param.8), kind=kOutput, calls=%fused_computation.35 | convolution fusion | flops 3758096384 | bytes 32374784 | tf_op jit(solution)/shard_map/dot_general | solution.py:64
  75.9 19.7 %all-to-all-done = bf16[24,16,1792]{2,0,1:T(8,128)(2,1)} async-done(((bf16[24,16,1792]{2,0,1:T(8,128)(2,1)}), bf16[24,16,1792]{2,0,1:T(8,128)(2,1)}, u32[]{:S(2)}, u32[]{:S(2)}) %all-to-all-start) | async-done | bytes 1376288 | tf_op jit(solution)/shard_map/all_to_all | solution.py:63
  95.6 2.8 %fusion.1 = bf16[128,1792]{1,0:T(8,128)(2,1)} fusion(f32[128,1792]{1,0:T(8,128)} %fusion.18, bf16[384,1792]{1,0:T(8,128)(2,1)} %bitcast.4, s32[128]{0:T(128)S(1)} %get-tuple-element.9), kind=kOutput, calls=%fused_computation.3 | convolution fusion | flops 176668672 | bytes 2753024 | tf_op jit(solution)/shard_map/dot_general | solution.py:70
  (3 shorter events, 0.0 us)
Async XLA Ops:
  6.5 44.1 %copy-start = (bf16[1,64,8192]{2,1,0:T(8,128)(2,1)S(1)}, bf16[1,64,8192]{2,1,0:T(8,128)(2,1)}, u32[]{:S(2)}) copy-start(bf16[1,64,8192]{2,1,0:T(8,128)(2,1)} %param.9) | copy-start | bytes 3145732
  6.5 44.1 %all-gather.2.cloned.1.call-start = ((), (), s32[]{:S(2)}) async-start(), calls=%async_computation.1 | async-start | bytes 2228224 | tf_op jit(solution)/shard_map/all_gather | solution.py:44
  55.8 7.7 %copy-start.1 = (bf16[128,8192]{1,0:T(8,128)(2,1)S(1)}, bf16[128,8192]{1,0:T(8,128)(2,1)}, u32[]{:S(2)}) copy-start(bf16[128,8192]{1,0:T(8,128)(2,1)} %all-gather.2.cloned.1.call-done) | copy-start | bytes 6291460
  57.0 38.6 %all-to-all-start = ((bf16[24,16,1792]{2,0,1:T(8,128)(2,1)}), bf16[24,16,1792]{2,0,1:T(8,128)(2,1)}, u32[]{:S(2)}, u32[]{:S(2)}) async-start(bf16[24,16,1792]{2,0,1:T(8,128)(2,1)} %bitcast.20), calls=%async_computation | async-start | bytes 2752512 | tf_op jit(solution)/shard_map/all_to_all | solution.py:63
Sparse Core Ops, SparseCore 0:
  9.5 41.0 all-gather.1

commit v2 on v1

--- a/solution.py
+++ b/solution.py
@@ -4,6 +4,21 @@
 from jax.sharding import PartitionSpec as P
 
 ROW_CAP = 24
+
+
+def gather(block):
+    if lax.axis_size("pool") != 16:
+        return lax.all_gather(block, "pool", axis=0, tiled=True), None
+
+    def swap(value, bits):
+        return lax.ppermute(value, "pool", [(i, i ^ bits) for i in range(16)])
+
+    far, near, side = swap(block, 8), swap(block, 4), swap(block, 2)
+    far_near, far_diagonal = swap(far, 4), swap(far, 6)
+    across = swap(jnp.concatenate([near, far]), 2)
+    half = jnp.concatenate([block, far, near, side, far_near, far_diagonal, across])
+    keys = (0, 8, 4, 2, 12, 14, 6, 10)
+    return jnp.concatenate([half, swap(half, 1)]), keys + tuple(k ^ 1 for k in keys)
 
 
 def on_device(
@@ -41,17 +56,23 @@
     before = jnp.arange(rows)[None, :] < jnp.arange(rows)[:, None]
     place = jnp.sum((before & (owner[:, None] == owner[None, :])).astype(jnp.int32), axis=1)
 
-    x = lax.all_gather(normed_input_rows, "pool", axis=0, tiled=True)
+    x, keys = gather(normed_input_rows)
+    each = normed_input_rows.shape[0]
+    block = jnp.asarray(keys, jnp.int32) ^ member if keys else jnp.arange(npool, dtype=jnp.int32)
+    actual = (block[:, None] * each + jnp.arange(each, dtype=jnp.int32)[None, :]).reshape(rows)
+    order = actual[:, None] == jnp.arange(rows, dtype=jnp.int32)[None, :]
+    slot_here = jnp.sum(jnp.where(order, row_slot[None, :], 0), axis=1)
+    place_here = jnp.sum(jnp.where(order, place[None, :], 0), axis=1)
     select = (
-        (place[None, :] == jnp.arange(ROW_CAP, dtype=jnp.int32)[:, None])
-        & (owner == member)[None, :]
+        (place_here[None, :] == jnp.arange(ROW_CAP, dtype=jnp.int32)[:, None])
+        & (slot_here // share == member)[None, :]
     ).astype(jnp.bfloat16)
     low = jnp.dot(
         x,
         adapter_down_factors.reshape(share * rank, -1).T,
         preferred_element_type=jnp.float32,
     ).astype(jnp.bfloat16)
-    which = row_slot - member * share
+    which = slot_here - member * share
     mine = which[:, None] == jnp.arange(share * rank, dtype=jnp.int32)[None, :] // rank
     low = jnp.where(mine, low, 0)
     chosen = jnp.dot(select, low, preferred_element_type=jnp.float32).astype(jnp.bfloat16)
@@ -61,6 +82,10 @@
         preferred_element_type=jnp.float32,
     ).astype(jnp.bfloat16)
     received = lax.all_to_all(terms, "pool", split_axis=1, concat_axis=0, tiled=True)
+    if keys:
+        x = jnp.dot(
+            order.T.astype(jnp.bfloat16), x, preferred_element_type=jnp.float32
+        ).astype(jnp.bfloat16)
     base = jnp.dot(x, gate_base_weight, preferred_element_type=jnp.float32)
     base, received = lax.optimization_barrier((base, received))
     pick = (

time: 106 us -> 71.8 us (0.68)
  the two profiles are of different devices: /device:TPU:13 before, /device:TPU:15 now
where the time goes in v2:
time: 71.8 us; the launch traced here: 71.5 us
  waiting for transfers between devices  25.9 us (36%)
  matrix products  19.8 us (28%)
  starting transfers between devices  16.2 us (23%)
  local copies, waits for them, and re-layouts  8.23 us (11%)
  other arithmetic  1.29 us (2%)
    all_to_all x1, waiting for transfers between devices, on_device(): lax.all_to_all(terms, 'pool', split_axis=1, concat_axis=0, tiled=True)  18.7 us
    dot_general x1, matrix products, on_device(): base = jnp.dot(x, gate_base_weight, preferred_element_type=jnp.float32)  13.4 us
    ppermute x7, starting transfers between devices, swap(): return lax.ppermute(value, 'pool', [(i, i ^ bits) for i in range(16)])  9.22 us
    ppermute x7, waiting for transfers between devices, swap(): return lax.ppermute(value, 'pool', [(i, i ^ bits) for i in range(16)])  7.25 us
    all_to_all x1, starting transfers between devices, on_device(): lax.all_to_all(terms, 'pool', split_axis=1, concat_axis=0, tiled=True)  6.94 us
    unnamed x14, local copies, waits for them, and re-layouts  4.95 us
    dot_general x1, matrix products, on_device(): delta = jnp.dot(pick, received, preferred_element_type=jnp.float32)  2.81 us
    dot_general x1, matrix products, on_device(): jnp.dot(chosen, adapter_up_factors.reshape(share * rank, -1), preferred_e...  2.65 us
  transfers between devices with their start and end apart: 8, of which 5 were waited for; matrix products, arithmetic and copies ran while one was open for 28% of the time, Pallas kernels for 0%

profile of v2, /device:TPU:15, one launch (start us, length us, event | category | flops | bytes accessed | tf_op | source)
XLA Modules:
  0.0 71.5 jit_solution(1412668390737982325)
XLA Ops:
  0.0 2.4 %collective-permute-start = (bf16[8,8192]{1,0:T(8,128)(2,1)}, bf16[8,8192]{1,0:T(8,128)(2,1)S(1)}, u32[]{:S(2)}, u32[]{:S(2)}) collective-permute-start(bf16[8,8192]{1,0:T(8,128)(2,1)} %param.8), channel_id=1, source_target_pairs={{0,8},{1,9},{2,10},{3,11},{4,12},{5,13},{6,14},{7,15},{8,0},{9,1},... | collective-permute-start | bytes 393224 | tf_op jit(solution)/shard_map/ppermute | solution.py:14
  2.4 0.2 collective-permute-start.1
  2.6 0.2 collective-permute-start.2
  2.8 1.6 %constant_dynamic-update-slice_fusion.6 = (bf16[64,8192]{1,0:T(8,128)(2,1)}, bf16[128,8192]{1,0:T(8,128)(2,1)S(1)}) fusion(bf16[8,8192]{1,0:T(8,128)(2,1)} %param.8), kind=kLoop, calls=%fused_computation.27 | loop fusion | bytes 393216
  4.4 0.7 xor_multiply_fusion
  5.1 3.6 %collective-permute-done = bf16[8,8192]{1,0:T(8,128)(2,1)S(1)} collective-permute-done((bf16[8,8192]{1,0:T(8,128)(2,1)}, bf16[8,8192]{1,0:T(8,128)(2,1)S(1)}, u32[]{:S(2)}, u32[]{:S(2)}) %collective-permute-start) | collective-permute-done | bytes 131104 | tf_op jit(solution)/shard_map/ppermute | solution.py:14
  8.7 0.3 collective-permute-start.5
  8.9 2.4 %collective-permute-start.4 = (bf16[8,8192]{1,0:T(8,128)(2,1)S(1)}, bf16[8,8192]{1,0:T(8,128)(2,1)S(1)}, u32[]{:S(2)}, u32[]{:S(2)}) collective-permute-start(bf16[8,8192]{1,0:T(8,128)(2,1)S(1)} %collective-permute-done), channel_id=1, source_target_pairs={{0,6},{1,7},{2,4},{3,5},{4,2},{5,3},{6,0},{7,1},{8,14},{9,15},{10,... | collective-permute-start | bytes 393224 | tf_op jit(solution)/shard_map/ppermute | solution.py:14
  11.4 0.7 constant_dynamic-update-slice_fusion.5
  12.0 0.7 constant_dynamic-update-slice_fusion.4
  12.7 0.7 constant_dynamic-update-slice_fusion.3
  13.4 0.7 constant_dynamic-update-slice_fusion.2
  14.0 1.7 %collective-permute-done.4 = bf16[8,8192]{1,0:T(8,128)(2,1)S(1)} collective-permute-done((bf16[8,8192]{1,0:T(8,128)(2,1)S(1)}, bf16[8,8192]{1,0:T(8,128)(2,1)S(1)}, u32[]{:S(2)}, u32[]{:S(2)}) %collective-permute-start.4) | collective-permute-done | bytes 131104 | tf_op jit(solution)/shard_map/ppermute | solution.py:14
  15.7 0.7 constant_dynamic-update-slice_fusion.1
  16.4 0.1 collective-permute-done.5
  16.5 0.7 %constant_dynamic-update-slice_fusion = (bf16[64,8192]{1,0:T(8,128)(2,1)}, bf16[128,8192]{1,0:T(8,128)(2,1)S(1)}) fusion(bf16[64,8192]{1,0:T(8,128)(2,1)} %get-tuple-element.13, bf16[16,8192]{1,0:T(8,128)(2,1)S(1)} %collective-permute-done.5, bf16[128,8192]{1,0:T(8,128)(2,1)S(1)} %get-tuple-element.14), kind=kLoop, calls=%fused_computation.21 | loop fusion | bytes 786432 | tf_op jit(solution)/shard_map/concatenate | solution.py:19
  17.2 3.7 %collective-permute-start.6 = (bf16[64,8192]{1,0:T(8,128)(2,1)}, bf16[64,8192]{1,0:T(8,128)(2,1)}, u32[]{:S(2)}, u32[]{:S(2)}) collective-permute-start(bf16[64,8192]{1,0:T(8,128)(2,1)} %get-tuple-element.11), channel_id=1, source_target_pairs={{0,1},{1,0},{2,3},{3,2},{4,5},{5,4},{6,7},{7,6},{8,9},{9,8},{10,11... | collective-permute-start | bytes 3145736 | tf_op jit(solution)/shard_map/ppermute | solution.py:14
  21.0 0.1 iota_add_fusion
  21.1 0.1 add.45
  21.2 0.1 select_reduce_fusion.3
  21.3 0.1 select_reduce_fusion.2
  21.4 0.2 convert_reduce_fusion
  21.5 0.2 select_reduce_fusion.1
  21.7 1.9 %collective-permute-done.6 = bf16[64,8192]{1,0:T(8,128)(2,1)} collective-permute-done((bf16[64,8192]{1,0:T(8,128)(2,1)}, bf16[64,8192]{1,0:T(8,128)(2,1)}, u32[]{:S(2)}, u32[]{:S(2)}) %collective-permute-start.6) | collective-permute-done | bytes 1048608 | tf_op jit(solution)/shard_map/ppermute | solution.py:14
  23.6 1.3 %constant_dynamic-update-slice_fusion.7 = bf16[128,8192]{1,0:T(8,128)(2,1)S(1)} fusion(bf16[128,8192]{1,0:T(8,128)(2,1)S(1)} %get-tuple-element.12, bf16[64,8192]{1,0:T(8,128)(2,1)} %collective-permute-done.6), kind=kLoop, calls=%fused_computation.28 | loop fusion | bytes 2097152 | tf_op jit(solution)/shard_map/concatenate | solution.py:21
  24.9 1.0 %fusion.5 = bf16[24,64]{1,0:T(8,128)(2,1)S(1)} fusion(bf16[128,8192]{1,0:T(8,128)(2,1)S(1)} %constant_dynamic-update-slice_fusion.7, bf16[1,64,8192]{2,1,0:T(8,128)(2,1)S(1)} %copy-done, s32[128]{0:T(128)S(1)} %broadcast_subtract_fusion, s32[64]{0:T(128)S(1)} %and_select_fusion, s32[128]{0:T(128)S(1)} %get-tuple-element.9, ...), kind=kOutput, calls=%fused_computation.10 | convolution fusion | flops 134643200 | bytes 3150208 | tf_op jit(solution)/shard_map/dot_general | solution.py:78
  25.9 2.6 %convolution_convert_fusion = bf16[24,28672]{1,0:T(8,128)(2,1)S(1)} fusion(bf16[24,64]{1,0:T(8,128)(2,1)S(1)} %fusion.5, bf16[1,64,28672]{2,1,0:T(8,128)(2,1)} %param.11), kind=kOutput, calls=%fused_computation | convolution fusion | flops 88768512 | bytes 5049344 | tf_op jit(solution)/shard_map/dot_general | solution.py:79
  28.5 1.2 %copy.13 = bf16[3,16,8,1792]{3,2,0,1:T(8,128)(2,1)} copy(bf16[3,16,8,1792]{3,2,1,0:T(8,128)(2,1)S(1)} %bitcast.21) | data formatting | bytes 2752512 | tf_op jit(solution)/shard_map/all_to_all | solution.py:84
  29.7 6.9 %all-to-all-start = ((bf16[24,16,1792]{2,0,1:T(8,128)(2,1)}), bf16[24,16,1792]{2,0,1:T(8,128)(2,1)}, u32[]{:S(2)}, u32[]{:S(2)}) async-start(bf16[24,16,1792]{2,0,1:T(8,128)(2,1)} %bitcast.20), calls=%async_computation | async-start | bytes 2752512 | tf_op jit(solution)/shard_map/all_to_all | solution.py:84
  36.6 13.4 %fusion.2 = f32[128,1792]{1,0:T(8,128)} fusion(bf16[8192,1792]{1,0:T(8,128)(2,1)} %param.9, bf16[128,8192]{1,0:T(8,128)(2,1)S(1)} %constant_dynamic-update-slice_fusion.7, s32[128]{0:T(128)S(1)} %add.45), kind=kOutput, calls=%fused_computation.5 | convolution fusion | flops 4027596800 | bytes 32375296 | tf_op jit(solution)/shard_map/dot_general | solution.py:89
  50.0 18.7 %all-to-all-done = bf16[24,16,1792]{2,0,1:T(8,128)(2,1)} async-done(((bf16[24,16,1792]{2,0,1:T(8,128)(2,1)}), bf16[24,16,1792]{2,0,1:T(8,128)(2,1)}, u32[]{:S(2)}, u32[]{:S(2)}) %all-to-all-start) | async-done | bytes 1376288 | tf_op jit(solution)/shard_map/all_to_all | solution.py:84
  68.7 2.8 %fusion.1 = bf16[128,1792]{1,0:T(8,128)(2,1)} fusion(f32[128,1792]{1,0:T(8,128)} %fusion.2, bf16[384,1792]{1,0:T(8,128)(2,1)} %bitcast.4, s32[128]{0:T(128)S(1)} %multiply_add_fusion), kind=kOutput, calls=%fused_computation.4 | convolution fusion | flops 176668672 | bytes 2753024 | tf_op jit(solution)/shard_map/dot_general | solution.py:95
  (17 shorter events, 0.1 us)
Async XLA Ops:
  0.0 24.9 %copy-start = (bf16[1,64,8192]{2,1,0:T(8,128)(2,1)S(1)}, bf16[1,64,8192]{2,1,0:T(8,128)(2,1)}, u32[]{:S(2)}) copy-start(bf16[1,64,8192]{2,1,0:T(8,128)(2,1)} %param.10) | copy-start | bytes 3145732
  0.0 21.2 %copy-start.2 = (s32[32,1]{0,1:T(1,128)S(1)}, s32[32,1]{0,1:T(1,128)}, u32[]{:S(2)}) copy-start(s32[32,1]{0,1:T(1,128)} %param.12) | copy-start | bytes 388
  0.0 21.2 %copy-start.1 = (s32[16]{0:T(128)S(1)}, s32[16]{0:T(128)}, u32[]{:S(2)}) copy-start(s32[16]{0:T(128)} %param.14) | copy-start | bytes 196
  0.0 21.3 %copy-start.3 = (s32[128]{0:T(128)S(1)}, s32[128]{0:T(128)}, u32[]{:S(2)}) copy-start(s32[128]{0:T(128)} %param.13) | copy-start | bytes 1540
  0.0 8.6 %collective-permute-start = (bf16[8,8192]{1,0:T(8,128)(2,1)}, bf16[8,8192]{1,0:T(8,128)(2,1)S(1)}, u32[]{:S(2)}, u32[]{:S(2)}) collective-permute-start(bf16[8,8192]{1,0:T(8,128)(2,1)} %param.8), channel_id=1, source_target_pairs={{0,8},{1,9},{2,10},{3,11},{4,12},{5,13},{6,14},{7,15},{8,0},{9,1},... | collective-permute-start | bytes 393224 | tf_op jit(solution)/shard_map/ppermute | solution.py:14
  2.4 6.2 %collective-permute-start.1 = (bf16[8,8192]{1,0:T(8,128)(2,1)}, bf16[8,8192]{1,0:T(8,128)(2,1)S(1)}, u32[]{:S(2)}, u32[]{:S(2)}) collective-permute-start(bf16[8,8192]{1,0:T(8,128)(2,1)} %param.8), channel_id=1, source_target_pairs={{0,4},{1,5},{2,6},{3,7},{4,0},{5,1},{6,2},{7,3},{8,12},{9,13},{10,... | collective-permute-start | bytes 393224 | tf_op jit(solution)/shard_map/ppermute | solution.py:14
  2.6 10.1 %collective-permute-start.2 = (bf16[8,8192]{1,0:T(8,128)(2,1)}, bf16[8,8192]{1,0:T(8,128)(2,1)S(1)}, u32[]{:S(2)}, u32[]{:S(2)}) collective-permute-start(bf16[8,8192]{1,0:T(8,128)(2,1)} %param.8), channel_id=1, source_target_pairs={{0,2},{1,3},{2,0},{3,1},{4,6},{5,7},{6,4},{7,5},{8,10},{9,11},{10,... | collective-permute-start | bytes 393224 | tf_op jit(solution)/shard_map/ppermute | solution.py:14
  8.7 7.9 %collective-permute-start.5 = (bf16[16,8192]{1,0:T(8,128)(2,1)S(1)}, bf16[16,8192]{1,0:T(8,128)(2,1)S(1)}, u32[]{:S(2)}, u32[]{:S(2)}) collective-permute-start(bf16[16,8192]{1,0:T(8,128)(2,1)S(1)} %pad_maximum_fusion), channel_id=1, source_target_pairs={{0,2},{1,3},{2,0},{3,1},{4,6},{5,7},{6,4},{7,5},{8,10},{9,11},{10,... | collective-permute-start | bytes 786440 | tf_op jit(solution)/shard_map/ppermute | solution.py:14
  8.9 4.4 %collective-permute-start.3 = (bf16[8,8192]{1,0:T(8,128)(2,1)S(1)}, bf16[8,8192]{1,0:T(8,128)(2,1)S(1)}, u32[]{:S(2)}, u32[]{:S(2)}) collective-permute-start(bf16[8,8192]{1,0:T(8,128)(2,1)S(1)} %collective-permute-done), channel_id=1, source_target_pairs={{0,4},{1,5},{2,6},{3,7},{4,0},{5,1},{6,2},{7,3},{8,12},{9,13},{10,... | collective-permute-start | bytes 393224 | tf_op jit(solution)/shard_map/ppermute | solution.py:14
  8.9 6.8 %collective-permute-start.4 = (bf16[8,8192]{1,0:T(8,128)(2,1)S(1)}, bf16[8,8192]{1,0:T(8,128)(2,1)S(1)}, u32[]{:S(2)}, u32[]{:S(2)}) collective-permute-start(bf16[8,8192]{1,0:T(8,128)(2,1)S(1)} %collective-permute-done), channel_id=1, source_target_pairs={{0,6},{1,7},{2,4},{3,5},{4,2},{5,3},{6,0},{7,1},{8,14},{9,15},{10,... | collective-permute-start | bytes 393224 | tf_op jit(solution)/shard_map/ppermute | solution.py:14
  17.2 6.4 %collective-permute-start.6 = (bf16[64,8192]{1,0:T(8,128)(2,1)}, bf16[64,8192]{1,0:T(8,128)(2,1)}, u32[]{:S(2)}, u32[]{:S(2)}) collective-permute-start(bf16[64,8192]{1,0:T(8,128)(2,1)} %get-tuple-element.11), channel_id=1, source_target_pairs={{0,1},{1,0},{2,3},{3,2},{4,5},{5,4},{6,7},{7,6},{8,9},{9,8},{10,11... | collective-permute-start | bytes 3145736 | tf_op jit(solution)/shard_map/ppermute | solution.py:14
  29.7 39.0 %all-to-all-start = ((bf16[24,16,1792]{2,0,1:T(8,128)(2,1)}), bf16[24,16,1792]{2,0,1:T(8,128)(2,1)}, u32[]{:S(2)}, u32[]{:S(2)}) async-start(bf16[24,16,1792]{2,0,1:T(8,128)(2,1)} %bitcast.20), calls=%async_computation | async-start | bytes 2752512 | tf_op jit(solution)/shard_map/all_to_all | solution.py:84

commit v3 on v1

v3 whole, which is shorter than its diff:
```python
import jax
import jax.numpy as jnp
from jax import lax
from jax.experimental import pallas as pl
from jax.experimental.pallas import tpu as pltpu
from jax.sharding import PartitionSpec as P

ROW_CAP = 24
CHIP_CAP = 32
CHIP_REST = 2 * ROW_CAP - CHIP_CAP


def slots_and_places(request_adapter_id, row_request, adapter_storage_slot, share):
    adapters = adapter_storage_slot.shape[0]
    requests = request_adapter_id.shape[0]
    request_slot = jnp.sum(
        jnp.where(
            request_adapter_id == jnp.arange(adapters, dtype=jnp.int32)[None, :],
            adapter_storage_slot[None, :],
            0,
        ),
        axis=1,
    )
    row_slot = jnp.sum(
        jnp.where(
            row_request[:, None] == jnp.arange(requests, dtype=jnp.int32)[None, :],
            request_slot[None, :],
            0,
        ),
        axis=1,
    )
    rows = row_slot.shape[0]
    holder = row_slot // share
    before = jnp.arange(rows)[None, :] < jnp.arange(rows)[:, None]
    place = jnp.sum((before & (holder[:, None] == holder[None, :])).astype(jnp.int32), axis=1)
    return row_slot, place


def add_terms(base, received, holder, place, cap):
    at = jnp.where(place < cap, holder * cap + place, -1)
    pick = (at[:, None] == jnp.arange(received.shape[0], dtype=jnp.int32)[None, :]).astype(
        jnp.bfloat16
    )
    return base + jnp.dot(pick, received, preferred_element_type=jnp.float32)


def any_pool(
    normed_input_rows,
    gate_base_weight,
    adapter_down_factors,
    adapter_up_factors,
    request_adapter_id,
    row_request,
    adapter_storage_slot,
):
    member = lax.axis_index("pool")
    share, rank = adapter_down_factors.shape[:2]
    row_slot, place = slots_and_places(
        request_adapter_id, row_request, adapter_storage_slot, share
    )
    owner = row_slot // share
    cap = share * ROW_CAP
    x = lax.all_gather(normed_input_rows, "pool", axis=0, tiled=True)
    select = (
        (place[None, :] == jnp.arange(cap, dtype=jnp.int32)[:, None])
        & (owner == member)[None, :]
    ).astype(jnp.bfloat16)
    low = jnp.dot(
        x,
        adapter_down_factors.reshape(share * rank, -1).T,
        preferred_element_type=jnp.float32,
    ).astype(jnp.bfloat16)
    which = row_slot - member * share
    mine = which[:, None] == jnp.arange(share * rank, dtype=jnp.int32)[None, :] // rank
    low = jnp.where(mine, low, 0)
    chosen = jnp.dot(select, low, preferred_element_type=jnp.float32).astype(jnp.bfloat16)
    terms = jnp.dot(
        chosen,
        adapter_up_factors.reshape(share * rank, -1),
        preferred_element_type=jnp.float32,
    ).astype(jnp.bfloat16)
    received = lax.all_to_all(terms, "pool", split_axis=1, concat_axis=0, tiled=True)
    base = jnp.dot(x, gate_base_weight, preferred_element_type=jnp.float32)
    base, received = lax.optimization_barrier((base, received))
    return add_terms(base, received, owner, place, cap).astype(jnp.bfloat16)


def up_kernel(core, select, low_mine, low_theirs, up_mine, up_theirs, out, mine, theirs):
    rank = up_mine.shape[0]

    @pl.when(pl.program_id(0) == 0)
    def _():
        def pick(which, rows, low):
            return jnp.dot(select[which, rows], low, preferred_element_type=jnp.float32)

        mine[...] = (
            pick(0, 0, low_mine[:, :rank]) + pick(0, 1, low_theirs[:, rank:])
        ).astype(jnp.bfloat16)
        theirs[...] = (
            pick(1, 0, low_mine[:, rank:]) + pick(1, 1, low_theirs[:, :rank])
        ).astype(jnp.bfloat16)

    out[...] = (
        jnp.dot(mine[...], up_mine[...], preferred_element_type=jnp.float32)
        + jnp.dot(theirs[...], up_theirs[...], preferred_element_type=jnp.float32)
    ).astype(jnp.bfloat16)


def up_terms(core, select, low_mine, low_theirs, up_mine, up_theirs, chips, width):
    cap = select.shape[2]
    rank = up_mine.shape[0]

    def whole(shape):
        return pl.BlockSpec(shape, lambda j, core: (0,) * len(shape))

    columns = pl.BlockSpec((rank, width), lambda j, core: (0, 2 * j + core[0]))
    return pl.pallas_call(
        up_kernel,
        grid_spec=pltpu.PrefetchScalarGridSpec(
            num_scalar_prefetch=1,
            grid=(chips,),
            in_specs=[
                whole(select.shape),
                whole(low_mine.shape),
                whole(low_theirs.shape),
                columns,
                columns,
            ],
            out_specs=pl.BlockSpec((cap, width), lambda j, core: (j, 0)),
            scratch_shapes=[pltpu.VMEM((cap, rank), jnp.bfloat16)] * 2,
        ),
        out_shape=jax.ShapeDtypeStruct((chips * cap, width), jnp.bfloat16),
        cost_estimate=pl.CostEstimate(
            flops=4 * cap * rank * chips * width,
            bytes_accessed=4 * rank * chips * width + 2 * cap * chips * width,
            transcendentals=0,
        ),
        name="up_terms",
    )(core, select, low_mine, low_theirs, up_mine, up_theirs)


def chip_pool(
    normed_input_rows,
    gate_base_weight,
    adapter_down_factors,
    adapter_up_factors,
    request_adapter_id,
    row_request,
    adapter_storage_slot,
):
    npool, chips = 16, 8
    member = lax.axis_index("pool")
    core = member & 1
    width = gate_base_weight.shape[1]
    each = normed_input_rows.shape[0]
    rows = row_request.shape[0]

    def swap(value, bits):
        return lax.ppermute(value, "pool", [(i, i ^ bits) for i in range(npool)])

    far = swap(normed_input_rows, 8)
    near = swap(normed_input_rows, 4)
    side = swap(normed_input_rows, 2)
    far_near, far_diagonal = swap(far, 4), swap(far, 6)
    across = swap(jnp.concatenate([near, far]), 2)
    half = jnp.concatenate(
        [normed_input_rows, far, near, side, far_near, far_diagonal, across]
    )
    keys = jnp.asarray((0, 8, 4, 2, 12, 14, 6, 10), jnp.int32)
    down_mine, up_mine = adapter_down_factors[0], adapter_up_factors[0]
    down_theirs, up_theirs = swap(down_mine, 1), swap(up_mine, 1)

    row_slot, place = slots_and_places(
        request_adapter_id, row_request, adapter_storage_slot, 2
    )
    chip = row_slot // 2
    block = jnp.concatenate([keys ^ member, keys ^ member ^ 1])
    actual = (block[:, None] * each + jnp.arange(each, dtype=jnp.int32)[None, :]).reshape(rows)
    order = actual[:, None] == jnp.arange(rows, dtype=jnp.int32)[None, :]
    slot_here = jnp.sum(jnp.where(order, row_slot[None, :], 0), axis=1)
    place_here = jnp.sum(jnp.where(order, place[None, :], 0), axis=1)

    def selection(first, count):
        slots = (member ^ jnp.arange(2, dtype=jnp.int32))[:, None, None, None]
        places = (first + jnp.arange(count, dtype=jnp.int32))[None, None, :, None]
        return (
            (slot_here.reshape(1, 2, 1, -1) == slots)
            & (place_here.reshape(1, 2, 1, -1) == places)
        ).astype(jnp.bfloat16)

    low_mine = jnp.dot(
        half, jnp.concatenate([down_mine, down_theirs]).T, preferred_element_type=jnp.float32
    ).astype(jnp.bfloat16)
    low_theirs = swap(low_mine, 1)
    half, low_theirs = lax.optimization_barrier((half, low_theirs))

    def exchange(first, count):
        terms = up_terms(
            core.reshape(1),
            selection(first, count),
            low_mine,
            low_theirs,
            up_mine,
            up_theirs,
            chips,
            width,
        )
        return lax.all_to_all(
            terms,
            "pool",
            split_axis=0,
            concat_axis=0,
            tiled=True,
            axis_index_groups=[[2 * i + c for i in range(chips)] for c in range(2)],
        )

    received = exchange(0, CHIP_CAP)
    x = jnp.concatenate([half, swap(half, 1)])
    x = jnp.dot(
        order.T.astype(jnp.bfloat16), x, preferred_element_type=jnp.float32
    ).astype(jnp.bfloat16)
    base = jnp.dot(x, gate_base_weight, preferred_element_type=jnp.float32)
    base, received = lax.optimization_barrier((base, received))

    def all_placed(base):
        return add_terms(base, received, chip, place, CHIP_CAP).astype(jnp.bfloat16)

    def some_left(base):
        rest = exchange(CHIP_CAP, CHIP_REST)
        rest_place = jnp.where(place < CHIP_CAP, CHIP_REST, place - CHIP_CAP)
        return all_placed(add_terms(base, rest, chip, rest_place, CHIP_REST))

    return lax.cond(jnp.max(place) < CHIP_CAP, all_placed, some_left, base)


def solution(mesh):
    in_specs = (
        P(("groups", "pool"), None),
        P(None, "pool"),
        P(("groups", "pool"), None, None),
        P(("groups", "pool"), None, None),
        P("groups", None),
        P("groups"),
        P("groups"),
    )
    out_specs = P("groups", "pool")

    def on_device(*blocks):
        width, share = blocks[1].shape[1], blocks[2].shape[0]
        chip_wise = mesh.shape["pool"] == 16 and width % 128 == 0 and share == 1
        return (chip_pool if chip_wise else any_pool)(*blocks)

    return jax.shard_map(
        on_device, mesh=mesh, in_specs=in_specs, out_specs=out_specs, check_vma=False
    )
```

time: 106 us -> 63.7 us (0.60)
  the two profiles are of different devices: /device:TPU:13 before, /device:TPU:0 now
where the time goes in v3:
time: 63.7 us; the launch traced here: 63.3 us
  waiting for transfers between devices  17.9 us (28%)
  starting transfers between devices  16.5 us (26%)
  matrix products  15.4 us (24%)
  Pallas kernels  6.75 us (11%)
  other arithmetic  4.04 us (6%)
  local copies, waits for them, and re-layouts  1.99 us (3%)
  between operations  0.81 us (1%)
    dot_general x1, matrix products, chip_pool(): base = jnp.dot(x, gate_base_weight, preferred_element_type=jnp.float32)  12.7 us
    ppermute x10, starting transfers between devices, swap(): return lax.ppermute(value, 'pool', [(i, i ^ bits) for i in range(npool)])  11.9 us
    all_to_all x1, waiting for transfers between devices, exchange(): lax.all_to_all(terms, 'pool', split_axis=0, concat_axis=0, tiled=True, ax...  10.5 us
    ppermute x10, waiting for transfers between devices, swap(): return lax.ppermute(value, 'pool', [(i, i ^ bits) for i in range(npool)])  7.4 us
    pallas_call x1, Pallas kernels, up_terms(): pl.pallas_call(up_kernel, grid_spec=pltpu.PrefetchScalarGridSpec(num_scal...  6.75 us
    all_to_all x1, starting transfers between devices, exchange(): lax.all_to_all(terms, 'pool', split_axis=0, concat_axis=0, tiled=True, ax...  4.59 us
    dot_general x1, matrix products, chip_pool(): jnp.dot(half, jnp.concatenate([down_mine, down_theirs]).T, preferred_elem...  2.38 us
    unnamed x8, local copies, waits for them, and re-layouts  1.73 us
  transfers between devices with their start and end apart: 11, of which 4 were waited for; matrix products, arithmetic and copies ran while one was open for 32% of the time, Pallas kernels for 11%

profile of v3, /device:TPU:0, one launch (start us, length us, event | category | flops | bytes accessed | tf_op | source)
XLA Modules:
  0.0 63.3 jit_solution(12667463713605517053)
XLA Ops:
  0.0 3.0 %collective-permute-start.1 = (bf16[8,8192]{1,0:T(8,128)(2,1)}, bf16[8,8192]{1,0:T(8,128)(2,1)S(1)}, u32[]{:S(2)}, u32[]{:S(2)}) collective-permute-start(bf16[8,8192]{1,0:T(8,128)(2,1)} %param.10), channel_id=1, source_target_pairs={{0,4},{1,5},{2,6},{3,7},{4,0},{5,1},{6,2},{7,3},{8,12},{9,13},{10,... | collective-permute-start | bytes 393224 | tf_op jit(solution)/shard_map/ppermute | solution.py:159
  3.0 2.6 %collective-permute-start = (bf16[8,8192]{1,0:T(8,128)(2,1)}, bf16[8,8192]{1,0:T(8,128)(2,1)S(1)}, u32[]{:S(2)}, u32[]{:S(2)}) collective-permute-start(bf16[8,8192]{1,0:T(8,128)(2,1)} %param.10), channel_id=1, source_target_pairs={{0,8},{1,9},{2,10},{3,11},{4,12},{5,13},{6,14},{7,15},{8,0},{9,1},... | collective-permute-start | bytes 393224 | tf_op jit(solution)/shard_map/ppermute | solution.py:159
  5.6 1.5 %collective-permute-start.2 = (bf16[8,8192]{1,0:T(8,128)(2,1)}, bf16[8,8192]{1,0:T(8,128)(2,1)S(1)}, u32[]{:S(2)}, u32[]{:S(2)}) collective-permute-start(bf16[8,8192]{1,0:T(8,128)(2,1)} %param.10), channel_id=1, source_target_pairs={{0,2},{1,3},{2,0},{3,1},{4,6},{5,7},{6,4},{7,5},{8,10},{9,11},{10,... | collective-permute-start | bytes 393224 | tf_op jit(solution)/shard_map/ppermute | solution.py:159
  7.1 0.5 collective-permute-start.8
  7.6 0.9 %constant_dynamic-update-slice_fusion.6 = bf16[64,8192]{1,0:T(8,128)(2,1)S(1)} fusion(bf16[8,8192]{1,0:T(8,128)(2,1)} %param.10), kind=kLoop, calls=%fused_computation.44 | loop fusion | bytes 262144
  8.6 0.8 %select_reduce_fusion.3 = s32[32]{0:T(128)S(1)} fusion(s32[16]{0:T(128)} %param.16, s32[32]{0:T(128)} %bitcast.24), kind=kLoop, calls=%fused_computation.48 | loop fusion | flops 1504 | bytes 320 | tf_op jit(solution)/shard_map/reduce_sum | solution.py:16
  9.3 0.7 %select_reduce_fusion.2 = s32[128]{0:T(128)S(1)} fusion(s32[32]{0:T(128)S(1)} %select_reduce_fusion.3, s32[128]{0:T(128)} %param.15), kind=kLoop, calls=%fused_computation.45 | loop fusion | flops 12160 | bytes 1152 | tf_op jit(solution)/shard_map/reduce_sum | solution.py:24
  10.1 0.7 %broadcast_xor_fusion.1 = (s32[8]{0:T(128)S(1)}, s32[8]{0:T(128)S(1)}) fusion(s32[8]{0:T(128)} %constant.45.clone, s32[]{:T(128)} %axis_index.12), kind=kLoop, calls=%fused_computation.58 | loop fusion | flops 16 | bytes 100 | tf_op jit(solution)/shard_map/xor | solution.py:177
  10.7 0.2 convert_reduce_fusion
  10.9 1.0 %collective-permute-done = bf16[8,8192]{1,0:T(8,128)(2,1)S(1)} collective-permute-done((bf16[8,8192]{1,0:T(8,128)(2,1)}, bf16[8,8192]{1,0:T(8,128)(2,1)S(1)}, u32[]{:S(2)}, u32[]{:S(2)}) %collective-permute-start) | collective-permute-done | bytes 131104 | tf_op jit(solution)/shard_map/ppermute | solution.py:159
  12.0 1.6 %collective-permute-start.5 = (bf16[16,8192]{1,0:T(8,128)(2,1)S(1)}, bf16[16,8192]{1,0:T(8,128)(2,1)S(1)}, u32[]{:S(2)}, u32[]{:S(2)}) collective-permute-start(bf16[16,8192]{1,0:T(8,128)(2,1)S(1)} %pad_maximum_fusion), channel_id=1, source_target_pairs={{0,2},{1,3},{2,0},{3,1},{4,6},{5,7},{6,4},{7,5},{8,10},{9,11},{10,... | collective-permute-start | bytes 786440 | tf_op jit(solution)/shard_map/ppermute | solution.py:159
  13.6 0.4 collective-permute-start.4
  14.0 1.7 %collective-permute-start.3 = (bf16[8,8192]{1,0:T(8,128)(2,1)S(1)}, bf16[8,8192]{1,0:T(8,128)(2,1)S(1)}, u32[]{:S(2)}, u32[]{:S(2)}) collective-permute-start(bf16[8,8192]{1,0:T(8,128)(2,1)S(1)} %collective-permute-done), channel_id=1, source_target_pairs={{0,4},{1,5},{2,6},{3,7},{4,0},{5,1},{6,2},{7,3},{8,12},{9,13},{10,... | collective-permute-start | bytes 393224 | tf_op jit(solution)/shard_map/ppermute | solution.py:159
  15.7 4.8 %collective-permute-done.3 = bf16[8,8192]{1,0:T(8,128)(2,1)S(1)} collective-permute-done((bf16[8,8192]{1,0:T(8,128)(2,1)S(1)}, bf16[8,8192]{1,0:T(8,128)(2,1)S(1)}, u32[]{:S(2)}, u32[]{:S(2)}) %collective-permute-start.3) | collective-permute-done | bytes 131104 | tf_op jit(solution)/shard_map/ppermute | solution.py:159
  20.5 1.5 %collective-permute-done.5 = bf16[16,8192]{1,0:T(8,128)(2,1)S(1)} collective-permute-done((bf16[16,8192]{1,0:T(8,128)(2,1)S(1)}, bf16[16,8192]{1,0:T(8,128)(2,1)S(1)}, u32[]{:S(2)}, u32[]{:S(2)}) %collective-permute-start.5) | collective-permute-done | bytes 262176 | tf_op jit(solution)/shard_map/ppermute | solution.py:159
  22.1 2.4 %fusion.13.low_mine = bf16[64,128]{1,0:T(8,128)(2,1)S(1)} fusion(bf16[64,8192]{1,0:T(8,128)(2,1)S(1)} %constant_dynamic-update-slice_fusion, bf16[64,8192]{1,0:T(8,128)(2,1)} %collective-permute-done.6, bf16[64,8192]{1,0:T(8,128)(2,1)} %bitcast.23), kind=kOutput, calls=%fused_computation.27 | convolution fusion | flops 138420224 | bytes 3162112 | tf_op jit(solution)/shard_map/dot_general | solution.py:191
  24.6 0.1 add_multiply_fusion
  24.6 0.6 reduce_max.9
  25.9 0.6 collective-permute-start.9
  26.6 0.1 add.58
  26.6 0.2 select_reduce_fusion
  26.8 0.1 eq.187
  26.9 0.1 eq.183
  27.0 0.1 broadcast_compare_fusion.2
  27.1 0.6 and_convert_fusion.1.select
  27.7 6.7 %up_terms.3 = bf16[256,1792]{1,0:T(8,128)(2,1)} custom-call(s32[1]{0:T(128)} %bitcast.6.core, bf16[2,2,32,64]{3,2,1,0:T(8,128)(2,1)} %and_convert_fusion.1.select, bf16[64,128]{1,0:T(8,128)(2,1)S(1)} %fusion.13.low_mine, bf16[64,128]{1,0:T(8,128)(2,1)S(1)} %collective-permute-done.7.low_theirs, bf16[64,28672]{1,0:T(8,128)(2,1)} %bitcast.15, ...), custom_call_target="tpu_custom_call" | custom-call | flops 117440512 | bytes 4587520 | tf_op jit(solution)/shard_map/up_terms/pallas_call | solution.py:117
  34.5 4.6 %all-to-all-start.1 = ((bf16[8,32,1792]{2,1,0:T(8,128)(2,1)}), bf16[8,32,1792]{2,1,0:T(8,128)(2,1)S(1)}, u32[]{:S(2)}, u32[]{:S(2)}) async-start(bf16[8,32,1792]{2,1,0:T(8,128)(2,1)} %bitcast.19), calls=%async_computation.1 | async-start | bytes 1835008 | tf_op jit(solution)/shard_map/all_to_all | solution.py:208
  39.1 12.7 %fusion.11 = f32[128,1792]{1,0:T(8,128)S(1)} fusion(bf16[8192,1792]{1,0:T(8,128)(2,1)} %param.11, bf16[64,8192]{1,0:T(8,128)(2,1)} %collective-permute-done.9, bf16[64,8192]{1,0:T(8,128)(2,1)S(1)} %constant_dynamic-update-slice_fusion, s32[128]{0:T(128)S(1)} %add.58), kind=kOutput, calls=%fused_computation.26 | convolution fusion | flops 4031791104 | bytes 32375296 | tf_op jit(solution)/shard_map/dot_general | solution.py:222
  51.8 10.5 %all-to-all-done.1 = bf16[8,32,1792]{2,1,0:T(8,128)(2,1)S(1)} async-done(((bf16[8,32,1792]{2,1,0:T(8,128)(2,1)}), bf16[8,32,1792]{2,1,0:T(8,128)(2,1)S(1)}, u32[]{:S(2)}, u32[]{:S(2)}) %all-to-all-start.1) | async-done | bytes 917536 | tf_op jit(solution)/shard_map/all_to_all | solution.py:208
  62.2 0.3 conditional.7
  62.2 0.3 convolution_add_fusion.2
  62.6 0.8 %copy-done = bf16[128,1792]{1,0:T(8,128)(2,1)} copy-done((bf16[128,1792]{1,0:T(8,128)(2,1)}, bf16[128,1792]{1,0:T(8,128)(2,1)S(1)}, u32[]{:S(2)}) %copy-start) | copy-done | bytes 458776
  (22 shorter events, 0.3 us)
Async XLA Ops:
  0.0 10.9 %collective-permute-start.1 = (bf16[8,8192]{1,0:T(8,128)(2,1)}, bf16[8,8192]{1,0:T(8,128)(2,1)S(1)}, u32[]{:S(2)}, u32[]{:S(2)}) collective-permute-start(bf16[8,8192]{1,0:T(8,128)(2,1)} %param.10), channel_id=1, source_target_pairs={{0,4},{1,5},{2,6},{3,7},{4,0},{5,1},{6,2},{7,3},{8,12},{9,13},{10,... | collective-permute-start | bytes 393224 | tf_op jit(solution)/shard_map/ppermute | solution.py:159
  3.0 8.9 %collective-permute-start = (bf16[8,8192]{1,0:T(8,128)(2,1)}, bf16[8,8192]{1,0:T(8,128)(2,1)S(1)}, u32[]{:S(2)}, u32[]{:S(2)}) collective-permute-start(bf16[8,8192]{1,0:T(8,128)(2,1)} %param.10), channel_id=1, source_target_pairs={{0,8},{1,9},{2,10},{3,11},{4,12},{5,13},{6,14},{7,15},{8,0},{9,1},... | collective-permute-start | bytes 393224 | tf_op jit(solution)/shard_map/ppermute | solution.py:159
  5.6 8.4 %collective-permute-start.2 = (bf16[8,8192]{1,0:T(8,128)(2,1)}, bf16[8,8192]{1,0:T(8,128)(2,1)S(1)}, u32[]{:S(2)}, u32[]{:S(2)}) collective-permute-start(bf16[8,8192]{1,0:T(8,128)(2,1)} %param.10), channel_id=1, source_target_pairs={{0,2},{1,3},{2,0},{3,1},{4,6},{5,7},{6,4},{7,5},{8,10},{9,11},{10,... | collective-permute-start | bytes 393224 | tf_op jit(solution)/shard_map/ppermute | solution.py:159
  7.1 14.9 %collective-permute-start.6 = (bf16[64,8192]{1,0:T(8,128)(2,1)}, bf16[64,8192]{1,0:T(8,128)(2,1)}, u32[]{:S(2)}, u32[]{:S(2)}) collective-permute-start(bf16[64,8192]{1,0:T(8,128)(2,1)} %bitcast.22), channel_id=1, source_target_pairs={{0,1},{1,0},{2,3},{3,2},{4,5},{5,4},{6,7},{7,6},{8,9},{9,8},{10,11... | collective-permute-start | bytes 3145736 | tf_op jit(solution)/shard_map/ppermute | solution.py:159
  7.1 20.6 %collective-permute-start.8 = (bf16[64,28672]{1,0:T(8,128)(2,1)}, bf16[64,28672]{1,0:T(8,128)(2,1)}, u32[]{:S(2)}, u32[]{:S(2)}) collective-permute-start(bf16[64,28672]{1,0:T(8,128)(2,1)} %bitcast.14), channel_id=1, source_target_pairs={{0,1},{1,0},{2,3},{3,2},{4,5},{5,4},{6,7},{7,6},{8,9},{9,8},{10,11... | collective-permute-start | bytes 11010056 | tf_op jit(solution)/shard_map/ppermute | solution.py:159
  12.0 10.1 %collective-permute-start.5 = (bf16[16,8192]{1,0:T(8,128)(2,1)S(1)}, bf16[16,8192]{1,0:T(8,128)(2,1)S(1)}, u32[]{:S(2)}, u32[]{:S(2)}) collective-permute-start(bf16[16,8192]{1,0:T(8,128)(2,1)S(1)} %pad_maximum_fusion), channel_id=1, source_target_pairs={{0,2},{1,3},{2,0},{3,1},{4,6},{5,7},{6,4},{7,5},{8,10},{9,11},{10,... | collective-permute-start | bytes 786440 | tf_op jit(solution)/shard_map/ppermute | solution.py:159
  13.6 6.9 %collective-permute-start.4 = (bf16[8,8192]{1,0:T(8,128)(2,1)S(1)}, bf16[8,8192]{1,0:T(8,128)(2,1)S(1)}, u32[]{:S(2)}, u32[]{:S(2)}) collective-permute-start(bf16[8,8192]{1,0:T(8,128)(2,1)S(1)} %collective-permute-done), channel_id=1, source_target_pairs={{0,6},{1,7},{2,4},{3,5},{4,2},{5,3},{6,0},{7,1},{8,14},{9,15},{10,... | collective-permute-start | bytes 393224 | tf_op jit(solution)/shard_map/ppermute | solution.py:159
  14.0 6.5 %collective-permute-start.3 = (bf16[8,8192]{1,0:T(8,128)(2,1)S(1)}, bf16[8,8192]{1,0:T(8,128)(2,1)S(1)}, u32[]{:S(2)}, u32[]{:S(2)}) collective-permute-start(bf16[8,8192]{1,0:T(8,128)(2,1)S(1)} %collective-permute-done), channel_id=1, source_target_pairs={{0,4},{1,5},{2,6},{3,7},{4,0},{5,1},{6,2},{7,3},{8,12},{9,13},{10,... | collective-permute-start | bytes 393224 | tf_op jit(solution)/shard_map/ppermute | solution.py:159
  24.5 1.4 %collective-permute-start.7 = (bf16[64,128]{1,0:T(8,128)(2,1)S(1)}, bf16[64,128]{1,0:T(8,128)(2,1)S(1)}, u32[]{:S(2)}, u32[]{:S(2)}) collective-permute-start(bf16[64,128]{1,0:T(8,128)(2,1)S(1)} %fusion.13.low_mine), channel_id=1, source_target_pairs={{0,1},{1,0},{2,3},{3,2},{4,5},{5,4},{6,7},{7,6},{8,9},{9,8},{10,11... | collective-permute-start | bytes 49160 | tf_op jit(solution)/shard_map/ppermute | solution.py:159
  25.9 13.1 %collective-permute-start.9 = (bf16[64,8192]{1,0:T(8,128)(2,1)S(1)}, bf16[64,8192]{1,0:T(8,128)(2,1)}, u32[]{:S(2)}, u32[]{:S(2)}) collective-permute-start(bf16[64,8192]{1,0:T(8,128)(2,1)S(1)} %constant_dynamic-update-slice_fusion), channel_id=1, source_target_pairs={{0,1},{1,0},{2,3},{3,2},{4,5},{5,4},{6,7},{7,6},{8,9},{9,8},{10,11... | collective-permute-start | bytes 3145736 | tf_op jit(solution)/shard_map/ppermute | solution.py:159
  34.5 27.7 %all-to-all-start.1 = ((bf16[8,32,1792]{2,1,0:T(8,128)(2,1)}), bf16[8,32,1792]{2,1,0:T(8,128)(2,1)S(1)}, u32[]{:S(2)}, u32[]{:S(2)}) async-start(bf16[8,32,1792]{2,1,0:T(8,128)(2,1)} %bitcast.19), calls=%async_computation.1 | async-start | bytes 1835008 | tf_op jit(solution)/shard_map/all_to_all | solution.py:208
  62.6 0.8 %copy-start = (bf16[128,1792]{1,0:T(8,128)(2,1)}, bf16[128,1792]{1,0:T(8,128)(2,1)S(1)}, u32[]{:S(2)}) copy-start(bf16[128,1792]{1,0:T(8,128)(2,1)S(1)} %get-tuple-element.93) | copy-start | bytes 1376260

commit v4 on v3

--- a/solution.py
+++ b/solution.py
@@ -85,58 +85,169 @@
     return add_terms(base, received, owner, place, cap).astype(jnp.bfloat16)
 
 
-def up_kernel(core, select, low_mine, low_theirs, up_mine, up_theirs, out, mine, theirs):
+KEYS = (0, 8, 4, 2, 12, 14, 6, 10)
+
+
+def rows_kernel(member, request_id, row_request, slots, select, select_rest, facts, most):
+    requests, adapters = request_id.shape[0], slots.shape[1]
+    rows = row_request.shape[1]
+    me = member[0]
+
+    def iota(shape, axis):
+        return lax.broadcasted_iota(jnp.int32, shape, axis)
+
+    def where_sum(mask, values, axis):
+        return jnp.sum(jnp.where(mask, values, 0), axis=axis, keepdims=True)
+
+    named = request_id[...] == iota((requests, adapters), 1)
+    request_slot = where_sum(named, slots[...], 1)
+    asked = row_request[...] == iota((requests, rows), 0)
+    slot = where_sum(asked, request_slot, 0)
+    down, along = iota((rows, rows), 0), iota((rows, rows), 1)
+    slot_down = where_sum(down == along, slot, 1)
+    same = (slot_down // 2 == slot // 2) & (down < along)
+    place = where_sum(same, jnp.ones((rows, rows), jnp.int32), 0)
+    place_down = where_sum(down == along, place, 1)
+
+    lane = iota((1, rows), 1)
+    side, lane = lane // (rows // 2), lane % (rows // 2)
+    each = rows // (2 * len(KEYS))
+    holder = jnp.zeros((1, rows), jnp.int32)
+    for i, key in enumerate(KEYS):
+        holder = jnp.where(lane // each == i, key, holder)
+    actual = ((holder ^ side) ^ me) * each + lane % each
+    slot_here = where_sum(down == actual, slot_down, 0)
+    place_here = where_sum(down == actual, place_down, 0)
+    for first, out in ((0, select), (CHIP_CAP, select_rest)):
+        count = out.shape[1]
+        placed = place_here == first + iota((count, rows), 0)
+        for which in range(2):
+            out[which] = jnp.where(placed & (slot_here == (me ^ which)), 1.0, 0.0).astype(
+                out.dtype
+            )
+    line = iota(facts.shape, 0)
+    facts[...] = jnp.where(line == 0, slot // 2, jnp.where(line == 1, place, actual))
+    most[0] = jnp.max(place)
+
+
+def row_facts(member, request_adapter_id, row_request, adapter_storage_slot):
+    rows = row_request.shape[0]
+    smem, vmem = pl.BlockSpec(memory_space=pltpu.SMEM), pl.BlockSpec(memory_space=pltpu.VMEM)
+    select, select_rest, facts, most = pl.pallas_call(
+        rows_kernel,
+        in_specs=[smem, vmem, vmem, vmem],
+        out_specs=[vmem, vmem, vmem, smem],
+        out_shape=[
+            jax.ShapeDtypeStruct((2, CHIP_CAP, rows), jnp.bfloat16),
+            jax.ShapeDtypeStruct((2, CHIP_REST, rows), jnp.bfloat16),
+            jax.ShapeDtypeStruct((8, rows), jnp.int32),
+            jax.ShapeDtypeStruct((1,), jnp.int32),
+        ],
+        name="row_facts",
+    )(
+        member.reshape(1),
+        request_adapter_id,
+        row_request.reshape(1, rows),
+        adapter_storage_slot.reshape(1, -1),
+    )
+    return select, select_rest, facts[0], facts[1], facts[2], most[0]
+
+
+def low_kernel(
+    core, half, down_mine, down_theirs, up_mine, up_theirs, low, columns, sems
+):
     rank = up_mine.shape[0]
-
-    @pl.when(pl.program_id(0) == 0)
-    def _():
-        def pick(which, rows, low):
-            return jnp.dot(select[which, rows], low, preferred_element_type=jnp.float32)
-
-        mine[...] = (
-            pick(0, 0, low_mine[:, :rank]) + pick(0, 1, low_theirs[:, rank:])
+    chips, _, width = columns.shape
+
+    def copy(j, which, source):
+        at = pl.multiple_of((2 * j + core[0]) * width, 128)
+        return pltpu.make_async_copy(
+            source.at[:, pl.ds(at, width)],
+            columns.at[j, pl.ds(which * rank, rank)],
+            sems.at[j, which],
+        )
+
+    copies = [
+        copy(j, which, source)
+        for j in range(chips)
+        for which, source in enumerate((up_mine, up_theirs))
+    ]
+    for c in copies:
+        c.start()
+    total = jnp.zeros(low.shape, jnp.float32)
+    depth = half.shape[1] // 8
+    for k in range(8):
+        part = slice(k * depth, (k + 1) * depth)
+        down = jnp.concatenate([down_mine[:, part], down_theirs[:, part]])
+        total += lax.dot_general(
+            half[:, part], down, (((1,), (1,)), ((), ())), preferred_element_type=jnp.float32
+        )
+    low[...] = total.astype(low.dtype)
+    for c in copies:
+        c.wait()
+
+
+def low_and_columns(core, half, down_mine, down_theirs, up_mine, up_theirs, chips, width):
+    rank = up_mine.shape[0]
+    vmem, anywhere = pl.BlockSpec(memory_space=pltpu.VMEM), pl.BlockSpec(memory_space=pl.ANY)
+    return pl.pallas_call(
+        low_kernel,
+        in_specs=[
+            pl.BlockSpec(memory_space=pltpu.SMEM),
+            vmem,
+            vmem,
+            vmem,
+            anywhere,
+            anywhere,
+        ],
+        out_specs=[vmem, vmem],
+        out_shape=[
+            pltpu.VMEM((half.shape[0], 2 * rank), jnp.bfloat16),
+            pltpu.VMEM((chips, 2 * rank, width), jnp.bfloat16),
+        ],
+        scratch_shapes=[pltpu.SemaphoreType.DMA((chips, 2))],
+        compiler_params=pltpu.CompilerParams(vmem_limit_bytes=16 * 2**20),
+        cost_estimate=pl.CostEstimate(
+            flops=4 * half.size * rank,
+            bytes_accessed=4 * rank * chips * width,
+            transcendentals=0,
+        ),
+        name="low_and_columns",
+    )(core, half, down_mine, down_theirs, up_mine, up_theirs)
+
+
+def up_kernel(select, low_mine, low_theirs, columns, out):
+    rank = columns.shape[1] // 2
+    cap = select.shape[1]
+    chosen = []
+    for which in range(2):
+        here = slice(which * rank, (which + 1) * rank)
+        there = slice((1 - which) * rank, (2 - which) * rank)
+        low = jnp.concatenate([low_mine[:, here], low_theirs[:, there]])
+        chosen.append(jnp.dot(select[which], low, preferred_element_type=jnp.float32))
+    low = jnp.concatenate(chosen, axis=1).astype(jnp.bfloat16)
+    for j in range(columns.shape[0]):
+        out[pl.ds(j * cap, cap), :] = jnp.dot(
+            low, columns[j], preferred_element_type=jnp.float32
         ).astype(jnp.bfloat16)
-        theirs[...] = (
-            pick(1, 0, low_mine[:, rank:]) + pick(1, 1, low_theirs[:, :rank])
-        ).astype(jnp.bfloat16)
-
-    out[...] = (
-        jnp.dot(mine[...], up_mine[...], preferred_element_type=jnp.float32)
-        + jnp.dot(theirs[...], up_theirs[...], preferred_element_type=jnp.float32)
-    ).astype(jnp.bfloat16)
-
-
-def up_terms(core, select, low_mine, low_theirs, up_mine, up_theirs, chips, width):
-    cap = select.shape[2]
-    rank = up_mine.shape[0]
-
-    def whole(shape):
-        return pl.BlockSpec(shape, lambda j, core: (0,) * len(shape))
-
-    columns = pl.BlockSpec((rank, width), lambda j, core: (0, 2 * j + core[0]))
+
+
+def up_terms(select, low_mine, low_theirs, columns):
+    cap = select.shape[1]
+    chips, depth, width = columns.shape
     return pl.pallas_call(
         up_kernel,
-        grid_spec=pltpu.PrefetchScalarGridSpec(
-            num_scalar_prefetch=1,
-            grid=(chips,),
-            in_specs=[
-                whole(select.shape),
-                whole(low_mine.shape),
-                whole(low_theirs.shape),
-                columns,
-                columns,
-            ],
-            out_specs=pl.BlockSpec((cap, width), lambda j, core: (j, 0)),
-            scratch_shapes=[pltpu.VMEM((cap, rank), jnp.bfloat16)] * 2,
-        ),
+        in_specs=[pl.BlockSpec(memory_space=pltpu.VMEM)] * 4,
+        out_specs=pl.BlockSpec(memory_space=pltpu.VMEM),
         out_shape=jax.ShapeDtypeStruct((chips * cap, width), jnp.bfloat16),
+        compiler_params=pltpu.CompilerParams(vmem_limit_bytes=16 * 2**20),
         cost_estimate=pl.CostEstimate(
-            flops=4 * cap * rank * chips * width,
-            bytes_accessed=4 * rank * chips * width + 2 * cap * chips * width,
+            flops=2 * cap * depth * chips * width,
+            bytes_accessed=2 * (depth + cap) * chips * width,
             transcendentals=0,
         ),
         name="up_terms",
-    )(core, select, low_mine, low_theirs, up_mine, up_theirs)
+    )(select, low_mine, low_theirs, columns)
 
 
 def chip_pool(
@@ -152,7 +263,6 @@
     member = lax.axis_index("pool")
     core = member & 1
     width = gate_base_weight.shape[1]
-    each = normed_input_rows.shape[0]
     rows = row_request.shape[0]
 
     def swap(value, bits):
@@ -166,45 +276,27 @@
     half = jnp.concatenate(
         [normed_input_rows, far, near, side, far_near, far_diagonal, across]
     )
-    keys = jnp.asarray((0, 8, 4, 2, 12, 14, 6, 10), jnp.int32)
     down_mine, up_mine = adapter_down_factors[0], adapter_up_factors[0]
     down_theirs, up_theirs = swap(down_mine, 1), swap(up_mine, 1)
 
-    row_slot, place = slots_and_places(
-        request_adapter_id, row_request, adapter_storage_slot, 2
-    )
-    chip = row_slot // 2
-    block = jnp.concatenate([keys ^ member, keys ^ member ^ 1])
-    actual = (block[:, None] * each + jnp.arange(each, dtype=jnp.int32)[None, :]).reshape(rows)
-    order = actual[:, None] == jnp.arange(rows, dtype=jnp.int32)[None, :]
-    slot_here = jnp.sum(jnp.where(order, row_slot[None, :], 0), axis=1)
-    place_here = jnp.sum(jnp.where(order, place[None, :], 0), axis=1)
-
-    def selection(first, count):
-        slots = (member ^ jnp.arange(2, dtype=jnp.int32))[:, None, None, None]
-        places = (first + jnp.arange(count, dtype=jnp.int32))[None, None, :, None]
-        return (
-            (slot_here.reshape(1, 2, 1, -1) == slots)
-            & (place_here.reshape(1, 2, 1, -1) == places)
-        ).astype(jnp.bfloat16)
-
-    low_mine = jnp.dot(
-        half, jnp.concatenate([down_mine, down_theirs]).T, preferred_element_type=jnp.float32
-    ).astype(jnp.bfloat16)
+    select, select_rest, chip, place, actual, most = row_facts(
+        member, request_adapter_id, row_request, adapter_storage_slot
+    )
+    half, select, select_rest, chip, place, actual, most = lax.optimization_barrier(
+        (half, select, select_rest, chip, place, actual, most)
+    )
+
+    def low_here(half):
+        return low_and_columns(
+            core.reshape(1), half, down_mine, down_theirs, up_mine, up_theirs, chips, width
+        )
+
+    low_mine, columns = low_here(half)
     low_theirs = swap(low_mine, 1)
-    half, low_theirs = lax.optimization_barrier((half, low_theirs))
-
-    def exchange(first, count):
-        terms = up_terms(
-            core.reshape(1),
-            selection(first, count),
-            low_mine,
-            low_theirs,
-            up_mine,
-            up_theirs,
-            chips,
-            width,
-        )
+    terms = up_terms(select, low_mine, low_theirs, columns)
+    half, terms = lax.optimization_barrier((half, terms))
+
+    def exchange(terms):
         return lax.all_to_all(
             terms,
             "pool",
@@ -214,11 +306,10 @@
             axis_index_groups=[[2 * i + c for i in range(chips)] for c in range(2)],
         )
 
-    received = exchange(0, CHIP_CAP)
+    received = exchange(terms)
     x = jnp.concatenate([half, swap(half, 1)])
-    x = jnp.dot(
-        order.T.astype(jnp.bfloat16), x, preferred_element_type=jnp.float32
-    ).astype(jnp.bfloat16)
+    order = (jnp.arange(rows, dtype=jnp.int32)[:, None] == actual[None, :]).astype(jnp.bfloat16)
+    x = jnp.dot(order, x, preferred_element_type=jnp.float32).astype(jnp.bfloat16)
     base = jnp.dot(x, gate_base_weight, preferred_element_type=jnp.float32)
     base, received = lax.optimization_barrier((base, received))
 
@@ -226,11 +317,12 @@
         return add_terms(base, received, chip, place, CHIP_CAP).astype(jnp.bfloat16)
 
     def some_left(base):
-        rest = exchange(CHIP_CAP, CHIP_REST)
+        low_mine, columns = low_here(half)
+        rest = exchange(up_terms(select_rest, low_mine, low_theirs, columns))
         rest_place = jnp.where(place < CHIP_CAP, CHIP_REST, place - CHIP_CAP)
         return all_placed(add_terms(base, rest, chip, rest_place, CHIP_REST))
 
-    return lax.cond(jnp.max(place) < CHIP_CAP, all_placed, some_left, base)
+    return lax.cond(most < CHIP_CAP, all_placed, some_left, base)
 
 
 def solution(mesh):

time: 63.7 us -> 60.9 us (0.956)
  other arithmetic: 4.04 us -> 0.02 us
  matrix products: 15.4 us -> 13 us
  local copies, waits for them, and re-layouts: 1.99 us -> 3.88 us
  Pallas kernels: 6.75 us -> 8.25 us
  waiting for transfers between devices: 17.9 us -> 19.4 us
  starting transfers between devices: 16.5 us -> 15.3 us
    dot_general x1 -> x0, matrix products: 2.38 us -> none  [chip_pool(): jnp.dot(half, jnp.concatenate([down_mine, down_theirs]).T, preferred_elem...]
    reduce_sum x4 -> x0, other arithmetic: 1.85 us -> none  [the longest x1 0.76 us: slots_and_places(): jnp.sum(jnp.where(request_adapter_id == jnp.arange(adapters, dtype=jnp.in...]
    pallas_call x1 -> x3, Pallas kernels: 6.75 us -> 8.25 us  [the longest x1 4.54 us: low_and_columns(): pl.pallas_call(low_kernel, in_specs=[pl.BlockSpec(memory_space=pltpu.SMEM...]
    unnamed x8 -> x13, local copies, waits for them, and re-layouts: 1.73 us -> 3.07 us
    ppermute x10, waiting for transfers between devices: 7.4 us -> 8.57 us  [swap(): return lax.ppermute(value, 'pool', [(i, i ^ bits) for i in range(npool)])]
    all_to_all x1, starting transfers between devices: 4.59 us -> 3.78 us  [exchange(): lax.all_to_all(terms, 'pool', split_axis=0, concat_axis=0, tiled=True, ax...]
    squeeze x0 -> x1, local copies, waits for them, and re-layouts: none -> 0.79 us  [row_facts(): return (select, select_rest, facts[0], facts[1], facts[2], most[0])]
    xor x2 -> x0, other arithmetic: 0.66 us -> none  [the longest x1 0.66 us: chip_pool(): block = jnp.concatenate([keys ^ member, keys ^ member ^ 1])]
  transfers between devices with their start and end apart: 11 -> 11, of which waited for: 4 -> 5; matrix products, arithmetic and copies ran while one was open for 32% -> 26% of each run, Pallas kernels for 11% -> 3%
where the time goes in v4:
time: 60.9 us; the launch traced here: 60.5 us
  waiting for transfers between devices  19.4 us (32%)
  starting transfers between devices  15.3 us (25%)
  matrix products  13 us (21%)
  Pallas kernels  8.25 us (14%)
  local copies, waits for them, and re-layouts  3.88 us (6%)
  between operations  0.73 us (1%)
    dot_general x1, matrix products, chip_pool(): base = jnp.dot(x, gate_base_weight, preferred_element_type=jnp.float32)  12.6 us
    ppermute x10, starting transfers between devices, swap(): return lax.ppermute(value, 'pool', [(i, i ^ bits) for i in range(npool)])  11.5 us
    all_to_all x1, waiting for transfers between devices, exchange(): lax.all_to_all(terms, 'pool', split_axis=0, concat_axis=0, tiled=True, ax...  10.8 us
    ppermute x10, waiting for transfers between devices, swap(): return lax.ppermute(value, 'pool', [(i, i ^ bits) for i in range(npool)])  8.57 us
    pallas_call x1, Pallas kernels, low_and_columns(): pl.pallas_call(low_kernel, in_specs=[pl.BlockSpec(memory_space=pltpu.SMEM...  4.54 us
    all_to_all x1, starting transfers between devices, exchange(): lax.all_to_all(terms, 'pool', split_axis=0, concat_axis=0, tiled=True, ax...  3.78 us
    unnamed x13, local copies, waits for them, and re-layouts  3.07 us
    pallas_call x1, Pallas kernels, row_facts(): pl.pallas_call(rows_kernel, in_specs=[smem, vmem, vmem, vmem], out_specs=...  1.85 us
  transfers between devices with their start and end apart: 11, of which 5 were waited for; matrix products, arithmetic and copies ran while one was open for 26% of the time, Pallas kernels for 3%

profile of v4, /device:TPU:0, one launch (start us, length us, event | category | flops | bytes accessed | tf_op | source)
XLA Modules:
  0.0 60.5 jit_solution(482774328109900350)
XLA Ops:
  0.0 4.0 %collective-permute-start = (bf16[8,8192]{1,0:T(8,128)(2,1)}, bf16[8,8192]{1,0:T(8,128)(2,1)S(1)}, u32[]{:S(2)}, u32[]{:S(2)}) collective-permute-start(bf16[8,8192]{1,0:T(8,128)(2,1)} %param.9), channel_id=1, source_target_pairs={{0,8},{1,9},{2,10},{3,11},{4,12},{5,13},{6,14},{7,15},{8,0},{9,1},... | collective-permute-start | bytes 393224 | tf_op jit(solution)/shard_map/ppermute | solution.py:269
  4.0 1.6 %collective-permute-start.1 = (bf16[8,8192]{1,0:T(8,128)(2,1)}, bf16[8,8192]{1,0:T(8,128)(2,1)S(1)}, u32[]{:S(2)}, u32[]{:S(2)}) collective-permute-start(bf16[8,8192]{1,0:T(8,128)(2,1)} %param.9), channel_id=1, source_target_pairs={{0,4},{1,5},{2,6},{3,7},{4,0},{5,1},{6,2},{7,3},{8,12},{9,13},{10,... | collective-permute-start | bytes 393224 | tf_op jit(solution)/shard_map/ppermute | solution.py:269
  5.6 1.5 %collective-permute-start.2 = (bf16[8,8192]{1,0:T(8,128)(2,1)}, bf16[8,8192]{1,0:T(8,128)(2,1)S(1)}, u32[]{:S(2)}, u32[]{:S(2)}) collective-permute-start(bf16[8,8192]{1,0:T(8,128)(2,1)} %param.9), channel_id=1, source_target_pairs={{0,2},{1,3},{2,0},{3,1},{4,6},{5,7},{6,4},{7,5},{8,10},{9,11},{10,... | collective-permute-start | bytes 393224 | tf_op jit(solution)/shard_map/ppermute | solution.py:269
  7.1 0.0 collective-permute-start.7
  7.1 0.5 collective-permute-start.6
  7.6 0.9 %constant_dynamic-update-slice_fusion.6 = bf16[64,8192]{1,0:T(8,128)(2,1)S(1)} fusion(bf16[8,8192]{1,0:T(8,128)(2,1)} %param.9), kind=kLoop, calls=%fused_computation.27 | loop fusion | bytes 262144
  8.6 1.3 %copy.10.request_id = s32[32,1]{1,0:T(8,128)} copy(s32[32,1]{0,1:T(1,128)} %param.13) | data formatting | bytes 256 | tf_op args[4]
  9.9 1.9 %row_facts.1 = (bf16[2,32,128]{2,1,0:T(8,128)(2,1)}, bf16[2,16,128]{2,1,0:T(8,128)(2,1)S(1)}, s32[8,128]{1,0:T(8,128)}, s32[1]{0:T(128)}) custom-call(s32[1]{0:T(128)} %bitcast.3.member, s32[32,1]{1,0:T(8,128)} %copy.10.request_id, s32[1,128]{1,0:T(1,128)} %bitcast.31, s32[1,16]{1,0:T(1,128)} %bitcast.32), custom_call_target="tpu_custom_call" | custom-call | tf_op jit(solution)/shard_map/row_facts/pallas_call | solution.py:136
  11.8 0.8 %slice_bitcast_fusion = (s32[128]{0:T(128)S(1)}, s32[128]{0:T(128)S(1)}, s32[128]{0:T(128)S(1)}) fusion(s32[8,128]{1,0:T(8,128)} %get-tuple-element.83), kind=kLoop, calls=%fused_computation.28 | loop fusion | bytes 3072 | tf_op jit(solution)/shard_map/squeeze | solution.py:153
  12.6 0.0 collective-permute-done
  12.6 0.0 collective-permute-done.1
  12.6 0.6 collective-permute-start.5
  13.2 0.7 %collective-permute-start.3 = (bf16[8,8192]{1,0:T(8,128)(2,1)S(1)}, bf16[8,8192]{1,0:T(8,128)(2,1)S(1)}, u32[]{:S(2)}, u32[]{:S(2)}) collective-permute-start(bf16[8,8192]{1,0:T(8,128)(2,1)S(1)} %collective-permute-done), channel_id=1, source_target_pairs={{0,4},{1,5},{2,6},{3,7},{4,0},{5,1},{6,2},{7,3},{8,12},{9,13},{10,... | collective-permute-start | bytes 393224 | tf_op jit(solution)/shard_map/ppermute | solution.py:269
  13.9 0.0 collective-permute-done.2
  13.9 2.3 %collective-permute-start.4 = (bf16[8,8192]{1,0:T(8,128)(2,1)S(1)}, bf16[8,8192]{1,0:T(8,128)(2,1)S(1)}, u32[]{:S(2)}, u32[]{:S(2)}) collective-permute-start(bf16[8,8192]{1,0:T(8,128)(2,1)S(1)} %collective-permute-done), channel_id=1, source_target_pairs={{0,6},{1,7},{2,4},{3,5},{4,2},{5,3},{6,0},{7,1},{8,14},{9,15},{10,... | collective-permute-start | bytes 393224 | tf_op jit(solution)/shard_map/ppermute | solution.py:269
  16.3 3.3 %collective-permute-done.3 = bf16[8,8192]{1,0:T(8,128)(2,1)S(1)} collective-permute-done((bf16[8,8192]{1,0:T(8,128)(2,1)S(1)}, bf16[8,8192]{1,0:T(8,128)(2,1)S(1)}, u32[]{:S(2)}, u32[]{:S(2)}) %collective-permute-start.3) | collective-permute-done | bytes 131104 | tf_op jit(solution)/shard_map/ppermute | solution.py:269
  19.6 2.6 %collective-permute-done.4 = bf16[8,8192]{1,0:T(8,128)(2,1)S(1)} collective-permute-done((bf16[8,8192]{1,0:T(8,128)(2,1)S(1)}, bf16[8,8192]{1,0:T(8,128)(2,1)S(1)}, u32[]{:S(2)}, u32[]{:S(2)}) %collective-permute-start.4) | collective-permute-done | bytes 131104 | tf_op jit(solution)/shard_map/ppermute | solution.py:269
  22.2 1.5 %collective-permute-done.5 = bf16[16,8192]{1,0:T(8,128)(2,1)S(1)} collective-permute-done((bf16[16,8192]{1,0:T(8,128)(2,1)S(1)}, bf16[16,8192]{1,0:T(8,128)(2,1)S(1)}, u32[]{:S(2)}, u32[]{:S(2)}) %collective-permute-start.5) | collective-permute-done | bytes 262176 | tf_op jit(solution)/shard_map/ppermute | solution.py:269
  23.7 0.0 collective-permute-done.7.up_theirs
  23.7 4.5 %low_and_columns.3 = (bf16[64,128]{1,0:T(8,128)(2,1)S(1)}, bf16[8,128,1792]{2,1,0:T(8,128)(2,1)S(1)}) custom-call(s32[1]{0:T(128)} %bitcast.10.core, bf16[64,8192]{1,0:T(8,128)(2,1)S(1)} %constant_dynamic-update-slice_fusion.half, bf16[64,8192]{1,0:T(8,128)(2,1)} %bitcast.28, bf16[64,8192]{1,0:T(8,128)(2,1)S(1)} %collective-permute-done.6.down_theirs, ...), custom_call_target="tpu_custom_call" | custom-call | flops 134217728 | bytes 3670016 | tf_op jit(solution)/shard_map/low_and_columns/pallas_call | solution.py:193
  28.3 0.1 collective-permute-start.8
  28.4 1.2 %collective-permute-done.8.low_theirs = bf16[64,128]{1,0:T(8,128)(2,1)S(1)} collective-permute-done((bf16[64,128]{1,0:T(8,128)(2,1)S(1)}, bf16[64,128]{1,0:T(8,128)(2,1)S(1)}, u32[]{:S(2)}, u32[]{:S(2)}) %collective-permute-start.8) | collective-permute-done | bytes 16416 | tf_op jit(solution)/shard_map/ppermute | solution.py:269
  29.6 1.9 %up_terms.3 = bf16[256,1792]{1,0:T(8,128)(2,1)} custom-call(bf16[2,32,128]{2,1,0:T(8,128)(2,1)S(1)} %copy-done, bf16[64,128]{1,0:T(8,128)(2,1)S(1)} %get-tuple-element.90.low_mine, bf16[64,128]{1,0:T(8,128)(2,1)S(1)} %collective-permute-done.8.low_theirs, bf16[8,128,1792]{2,1,0:T(8,128)(2,1)S(1)} %get-tuple-element.91.columns), custom_call_target="tpu_custom_call" | custom-call | flops 117440512 | bytes 4587520 | tf_op jit(solution)/shard_map/up_terms/pallas_call | solution.py:238
  31.4 0.2 collective-permute-start.9
  32.2 3.8 %all-to-all-start.1 = ((bf16[8,32,1792]{2,1,0:T(8,128)(2,1)}), bf16[8,32,1792]{2,1,0:T(8,128)(2,1)S(1)}, u32[]{:S(2)}, u32[]{:S(2)}) async-start(bf16[8,32,1792]{2,1,0:T(8,128)(2,1)} %bitcast.13), calls=%async_computation.1 | async-start | bytes 1835008 | tf_op jit(solution)/shard_map/all_to_all | solution.py:300
  35.9 0.0 collective-permute-done.9
  35.9 12.6 %fusion.7 = f32[128,1792]{1,0:T(8,128)S(1)} fusion(bf16[8192,1792]{1,0:T(8,128)(2,1)} %param.10, bf16[64,8192]{1,0:T(8,128)(2,1)} %collective-permute-done.9, bf16[64,8192]{1,0:T(8,128)(2,1)S(1)} %constant_dynamic-update-slice_fusion.half, s32[128]{0:T(128)S(1)} %get-tuple-element.94), kind=kOutput, calls=%fused_computation.17 | convolution fusion | flops 4031791104 | bytes 32375296 | tf_op jit(solution)/shard_map/dot_general | solution.py:313
  48.6 10.8 %all-to-all-done.1 = bf16[8,32,1792]{2,1,0:T(8,128)(2,1)S(1)} async-done(((bf16[8,32,1792]{2,1,0:T(8,128)(2,1)}), bf16[8,32,1792]{2,1,0:T(8,128)(2,1)S(1)}, u32[]{:S(2)}, u32[]{:S(2)}) %all-to-all-start.1) | async-done | bytes 917536 | tf_op jit(solution)/shard_map/all_to_all | solution.py:300
  59.4 0.3 conditional.7
  59.4 0.3 convolution_add_fusion.2
  59.8 0.0 copy-start.2
  59.8 0.8 %copy-done.2 = bf16[128,1792]{1,0:T(8,128)(2,1)} copy-done((bf16[128,1792]{1,0:T(8,128)(2,1)}, bf16[128,1792]{1,0:T(8,128)(2,1)S(1)}, u32[]{:S(2)}) %copy-start.2) | copy-done | bytes 458776
  (13 shorter events, 0.1 us)
Async XLA Ops:
  0.0 12.6 %collective-permute-start = (bf16[8,8192]{1,0:T(8,128)(2,1)}, bf16[8,8192]{1,0:T(8,128)(2,1)S(1)}, u32[]{:S(2)}, u32[]{:S(2)}) collective-permute-start(bf16[8,8192]{1,0:T(8,128)(2,1)} %param.9), channel_id=1, source_target_pairs={{0,8},{1,9},{2,10},{3,11},{4,12},{5,13},{6,14},{7,15},{8,0},{9,1},... | collective-permute-start | bytes 393224 | tf_op jit(solution)/shard_map/ppermute | solution.py:269
  4.0 8.5 %collective-permute-start.1 = (bf16[8,8192]{1,0:T(8,128)(2,1)}, bf16[8,8192]{1,0:T(8,128)(2,1)S(1)}, u32[]{:S(2)}, u32[]{:S(2)}) collective-permute-start(bf16[8,8192]{1,0:T(8,128)(2,1)} %param.9), channel_id=1, source_target_pairs={{0,4},{1,5},{2,6},{3,7},{4,0},{5,1},{6,2},{7,3},{8,12},{9,13},{10,... | collective-permute-start | bytes 393224 | tf_op jit(solution)/shard_map/ppermute | solution.py:269
  5.6 8.3 %collective-permute-start.2 = (bf16[8,8192]{1,0:T(8,128)(2,1)}, bf16[8,8192]{1,0:T(8,128)(2,1)S(1)}, u32[]{:S(2)}, u32[]{:S(2)}) collective-permute-start(bf16[8,8192]{1,0:T(8,128)(2,1)} %param.9), channel_id=1, source_target_pairs={{0,2},{1,3},{2,0},{3,1},{4,6},{5,7},{6,4},{7,5},{8,10},{9,11},{10,... | collective-permute-start | bytes 393224 | tf_op jit(solution)/shard_map/ppermute | solution.py:269
  7.1 16.6 %collective-permute-start.7 = (bf16[64,28672]{1,0:T(8,128)(2,1)}, bf16[64,28672]{1,0:T(8,128)(2,1)}, u32[]{:S(2)}, u32[]{:S(2)}) collective-permute-start(bf16[64,28672]{1,0:T(8,128)(2,1)} %bitcast.22), channel_id=1, source_target_pairs={{0,1},{1,0},{2,3},{3,2},{4,5},{5,4},{6,7},{7,6},{8,9},{9,8},{10,11... | collective-permute-start | bytes 11010056 | tf_op jit(solution)/shard_map/ppermute | solution.py:269
  7.1 16.6 %collective-permute-start.6 = (bf16[64,8192]{1,0:T(8,128)(2,1)}, bf16[64,8192]{1,0:T(8,128)(2,1)S(1)}, u32[]{:S(2)}, u32[]{:S(2)}) collective-permute-start(bf16[64,8192]{1,0:T(8,128)(2,1)} %bitcast.27), channel_id=1, source_target_pairs={{0,1},{1,0},{2,3},{3,2},{4,5},{5,4},{6,7},{7,6},{8,9},{9,8},{10,11... | collective-permute-start | bytes 3145736 | tf_op jit(solution)/shard_map/ppermute | solution.py:269
  12.6 11.1 %collective-permute-start.5 = (bf16[16,8192]{1,0:T(8,128)(2,1)S(1)}, bf16[16,8192]{1,0:T(8,128)(2,1)S(1)}, u32[]{:S(2)}, u32[]{:S(2)}) collective-permute-start(bf16[16,8192]{1,0:T(8,128)(2,1)S(1)} %pad_maximum_fusion), channel_id=1, source_target_pairs={{0,2},{1,3},{2,0},{3,1},{4,6},{5,7},{6,4},{7,5},{8,10},{9,11},{10,... | collective-permute-start | bytes 786440 | tf_op jit(solution)/shard_map/ppermute | solution.py:269
  13.2 6.4 %collective-permute-start.3 = (bf16[8,8192]{1,0:T(8,128)(2,1)S(1)}, bf16[8,8192]{1,0:T(8,128)(2,1)S(1)}, u32[]{:S(2)}, u32[]{:S(2)}) collective-permute-start(bf16[8,8192]{1,0:T(8,128)(2,1)S(1)} %collective-permute-done), channel_id=1, source_target_pairs={{0,4},{1,5},{2,6},{3,7},{4,0},{5,1},{6,2},{7,3},{8,12},{9,13},{10,... | collective-permute-start | bytes 393224 | tf_op jit(solution)/shard_map/ppermute | solution.py:269
  13.9 8.2 %collective-permute-start.4 = (bf16[8,8192]{1,0:T(8,128)(2,1)S(1)}, bf16[8,8192]{1,0:T(8,128)(2,1)S(1)}, u32[]{:S(2)}, u32[]{:S(2)}) collective-permute-start(bf16[8,8192]{1,0:T(8,128)(2,1)S(1)} %collective-permute-done), channel_id=1, source_target_pairs={{0,6},{1,7},{2,4},{3,5},{4,2},{5,3},{6,0},{7,1},{8,14},{9,15},{10,... | collective-permute-start | bytes 393224 | tf_op jit(solution)/shard_map/ppermute | solution.py:269
  23.7 4.6 %copy-start.1 = (bf16[64,8192]{1,0:T(8,128)(2,1)}, bf16[64,8192]{1,0:T(8,128)(2,1)S(1)}, u32[]{:S(2)}) copy-start(bf16[64,8192]{1,0:T(8,128)(2,1)S(1)} %collective-permute-done.6.down_theirs) | copy-start | bytes 3145732
  23.7 5.8 %copy-start = (bf16[2,32,128]{2,1,0:T(8,128)(2,1)S(1)}, bf16[2,32,128]{2,1,0:T(8,128)(2,1)}, u32[]{:S(2)}) copy-start(bf16[2,32,128]{2,1,0:T(8,128)(2,1)} %get-tuple-element.89.select) | copy-start | bytes 49156
  28.3 1.2 %collective-permute-start.8 = (bf16[64,128]{1,0:T(8,128)(2,1)S(1)}, bf16[64,128]{1,0:T(8,128)(2,1)S(1)}, u32[]{:S(2)}, u32[]{:S(2)}) collective-permute-start(bf16[64,128]{1,0:T(8,128)(2,1)S(1)} %get-tuple-element.90.low_mine), channel_id=1, source_target_pairs={{0,1},{1,0},{2,3},{3,2},{4,5},{5,4},{6,7},{7,6},{8,9},{9,8},{10,11... | collective-permute-start | bytes 49160 | tf_op jit(solution)/shard_map/ppermute | solution.py:269
  31.4 4.5 %collective-permute-start.9 = (bf16[64,8192]{1,0:T(8,128)(2,1)S(1)}, bf16[64,8192]{1,0:T(8,128)(2,1)}, u32[]{:S(2)}, u32[]{:S(2)}) collective-permute-start(bf16[64,8192]{1,0:T(8,128)(2,1)S(1)} %constant_dynamic-update-slice_fusion.half), channel_id=1, source_target_pairs={{0,1},{1,0},{2,3},{3,2},{4,5},{5,4},{6,7},{7,6},{8,9},{9,8},{10,11... | collective-permute-start | bytes 3145736 | tf_op jit(solution)/shard_map/ppermute | solution.py:269
  32.2 27.2 %all-to-all-start.1 = ((bf16[8,32,1792]{2,1,0:T(8,128)(2,1)}), bf16[8,32,1792]{2,1,0:T(8,128)(2,1)S(1)}, u32[]{:S(2)}, u32[]{:S(2)}) async-start(bf16[8,32,1792]{2,1,0:T(8,128)(2,1)} %bitcast.13), calls=%async_computation.1 | async-start | bytes 1835008 | tf_op jit(solution)/shard_map/all_to_all | solution.py:300
  59.8 0.8 %copy-start.2 = (bf16[128,1792]{1,0:T(8,128)(2,1)}, bf16[128,1792]{1,0:T(8,128)(2,1)S(1)}, u32[]{:S(2)}) copy-start(bf16[128,1792]{1,0:T(8,128)(2,1)S(1)} %get-tuple-element.119) | copy-start | bytes 1376260

commit v5 on v4

v5 whole, which is shorter than its diff:
```python
import functools

import jax
import jax.numpy as jnp
from jax import lax
from jax.experimental import pallas as pl
from jax.experimental.pallas import tpu as pltpu
from jax.sharding import PartitionSpec as P

ROW_CAP = 24
CHIP_CAP = 32
CHIP_REST = 2 * ROW_CAP - CHIP_CAP


def slots_and_places(request_adapter_id, row_request, adapter_storage_slot, share):
    adapters = adapter_storage_slot.shape[0]
    requests = request_adapter_id.shape[0]
    request_slot = jnp.sum(
        jnp.where(
            request_adapter_id == jnp.arange(adapters, dtype=jnp.int32)[None, :],
            adapter_storage_slot[None, :],
            0,
        ),
        axis=1,
    )
    row_slot = jnp.sum(
        jnp.where(
            row_request[:, None] == jnp.arange(requests, dtype=jnp.int32)[None, :],
            request_slot[None, :],
            0,
        ),
        axis=1,
    )
    rows = row_slot.shape[0]
    holder = row_slot // share
    before = jnp.arange(rows)[None, :] < jnp.arange(rows)[:, None]
    place = jnp.sum((before & (holder[:, None] == holder[None, :])).astype(jnp.int32), axis=1)
    return row_slot, place


def add_terms(base, received, holder, place, cap):
    at = jnp.where(place < cap, holder * cap + place, -1)
    pick = (at[:, None] == jnp.arange(received.shape[0], dtype=jnp.int32)[None, :]).astype(
        jnp.bfloat16
    )
    return base + jnp.dot(pick, received, preferred_element_type=jnp.float32)


def any_pool(
    normed_input_rows,
    gate_base_weight,
    adapter_down_factors,
    adapter_up_factors,
    request_adapter_id,
    row_request,
    adapter_storage_slot,
):
    member = lax.axis_index("pool")
    share, rank = adapter_down_factors.shape[:2]
    row_slot, place = slots_and_places(
        request_adapter_id, row_request, adapter_storage_slot, share
    )
    owner = row_slot // share
    cap = share * ROW_CAP
    x = lax.all_gather(normed_input_rows, "pool", axis=0, tiled=True)
    select = (
        (place[None, :] == jnp.arange(cap, dtype=jnp.int32)[:, None])
        & (owner == member)[None, :]
    ).astype(jnp.bfloat16)
    low = jnp.dot(
        x,
        adapter_down_factors.reshape(share * rank, -1).T,
        preferred_element_type=jnp.float32,
    ).astype(jnp.bfloat16)
    which = row_slot - member * share
    mine = which[:, None] == jnp.arange(share * rank, dtype=jnp.int32)[None, :] // rank
    low = jnp.where(mine, low, 0)
    chosen = jnp.dot(select, low, preferred_element_type=jnp.float32).astype(jnp.bfloat16)
    terms = jnp.dot(
        chosen,
        adapter_up_factors.reshape(share * rank, -1),
        preferred_element_type=jnp.float32,
    ).astype(jnp.bfloat16)
    received = lax.all_to_all(terms, "pool", split_axis=1, concat_axis=0, tiled=True)
    base = jnp.dot(x, gate_base_weight, preferred_element_type=jnp.float32)
    base, received = lax.optimization_barrier((base, received))
    return add_terms(base, received, owner, place, cap).astype(jnp.bfloat16)


KEYS = (0, 8, 4, 2, 12, 14, 6, 10)


def start_columns(core, up, outs, sems):
    chips, _, width = outs[0].shape
    copies = []
    for which, out in enumerate(outs):
        for j in range(chips):
            at = pl.multiple_of((2 * j + (core ^ which)) * width, 128)
            copies.append(
                pltpu.make_async_copy(up.at[:, pl.ds(at, width)], out.at[j], sems.at[which, j])
            )
    for c in copies:
        c.start()
    return copies


def columns_kernel(member, up, here, there, sems):
    for c in start_columns(member[0] & 1, up, (here, there), sems):
        c.wait()


def rows_kernel(
    requests,
    member,
    named,
    up,
    select,
    select_rest,
    pick,
    pick_rest,
    order,
    most,
    here,
    there,
    sems,
):
    rows = order.shape[0]
    me = member[0]
    copies = start_columns(me & 1, up, (here, there), sems)
    row_request = named[:, :rows]
    request_id, slots = named[:, rows : rows + requests], named[:, rows + requests :]
    adapters = slots.shape[1]

    def iota(shape, axis):
        return lax.broadcasted_iota(jnp.int32, shape, axis)

    def where_sum(mask, values, axis):
        return jnp.sum(jnp.where(mask, values, 0), axis=axis, keepdims=True)

    def one_hot(mask, out):
        return jnp.where(mask, 1.0, 0.0).astype(out.dtype)

    square = (requests, requests)
    request_down = where_sum(iota(square, 0) == iota(square, 1), request_id, 1)
    request_slot = where_sum(request_down == iota((requests, adapters), 1), slots, 1)
    slot = where_sum(row_request == iota((requests, rows), 0), request_slot, 0)
    down_rows, along = iota((rows, rows), 0), iota((rows, rows), 1)
    slot_down = where_sum(down_rows == along, slot, 1)
    same = (slot_down // 2 == slot // 2) & (down_rows < along)
    place = where_sum(same, jnp.ones((rows, rows), jnp.int32), 0)
    place_down = where_sum(down_rows == along, place, 1)

    lane = iota((1, rows), 1)
    side, lane = lane // (rows // 2), lane % (rows // 2)
    each = rows // (2 * len(KEYS))
    holder = jnp.zeros((1, rows), jnp.int32)
    for i, key in enumerate(KEYS):
        holder = jnp.where(lane // each == i, key, holder)
    actual = ((holder ^ side) ^ me) * each + lane % each
    order[...] = one_hot(down_rows == actual, order)
    slot_here = where_sum(down_rows == actual, slot_down, 0)
    place_here = where_sum(down_rows == actual, place_down, 0)
    for first, choice, back in ((0, select, pick), (CHIP_CAP, select_rest, pick_rest)):
        count = choice.shape[1]
        placed = place_here == first + iota((count, rows), 0)
        for which in range(2):
            choice[which] = one_hot(placed & (slot_here == (me ^ which)), choice)
        at = place_down - first
        at = jnp.where((at >= 0) & (at < count), slot_down // 2 * count + at, -1)
        back[...] = one_hot(at == iota(back.shape, 1), back)
    most[0] = jnp.max(place)
    for c in copies:
        c.wait()


def columns_shapes(up, chips):
    return [pltpu.VMEM((chips, up.shape[0], up.shape[1] // (2 * chips)), jnp.bfloat16)] * 2


def up_columns(member, up, chips):
    vmem = pl.BlockSpec(memory_space=pltpu.VMEM)
    return pl.pallas_call(
        columns_kernel,
        in_specs=[pl.BlockSpec(memory_space=pltpu.SMEM), pl.BlockSpec(memory_space=pl.ANY)],
        out_specs=[vmem] * 2,
        out_shape=columns_shapes(up, chips),
        scratch_shapes=[pltpu.SemaphoreType.DMA((2, chips))],
        compiler_params=pltpu.CompilerParams(vmem_limit_bytes=16 * 2**20),
        name="up_columns",
    )(member.reshape(1), up)


def prepare(member, request_adapter_id, row_request, adapter_storage_slot, up, chips):
    rows = row_request.shape[0]
    smem, vmem = pl.BlockSpec(memory_space=pltpu.SMEM), pl.BlockSpec(memory_space=pltpu.VMEM)
    return pl.pallas_call(
        functools.partial(rows_kernel, request_adapter_id.shape[0]),
        in_specs=[smem, vmem, pl.BlockSpec(memory_space=pl.ANY)],
        out_specs=[vmem] * 5 + [smem] + [vmem] * 2,
        out_shape=[
            pltpu.VMEM((2, CHIP_CAP, rows), jnp.bfloat16),
            jax.ShapeDtypeStruct((2, CHIP_REST, rows), jnp.bfloat16),
            pltpu.VMEM((rows, chips * CHIP_CAP), jnp.bfloat16),
            jax.ShapeDtypeStruct((rows, chips * CHIP_REST), jnp.bfloat16),
            pltpu.VMEM((rows, rows), jnp.bfloat16),
            jax.ShapeDtypeStruct((1,), jnp.int32),
            *columns_shapes(up, chips),
        ],
        scratch_shapes=[pltpu.SemaphoreType.DMA((2, chips))],
        compiler_params=pltpu.CompilerParams(vmem_limit_bytes=16 * 2**20),
        name="prepare",
    )(
        member.reshape(1),
        jnp.concatenate([row_request, request_adapter_id[:, 0], adapter_storage_slot])[None, :],
        up,
    )


def low_kernel(half, down_mine, down_theirs, low):
    total = jnp.zeros(low.shape, jnp.float32)
    depth = half.shape[1] // 8
    for k in range(8):
        part = slice(k * depth, (k + 1) * depth)
        down = jnp.concatenate([down_mine[:, part], down_theirs[:, part]])
        total += lax.dot_general(
            half[:, part], down, (((1,), (1,)), ((), ())), preferred_element_type=jnp.float32
        )
    low[...] = total.astype(low.dtype)


def low_values(half, down_mine, down_theirs):
    rank = down_mine.shape[0]
    vmem = pl.BlockSpec(memory_space=pltpu.VMEM)
    return pl.pallas_call(
        low_kernel,
        in_specs=[vmem] * 3,
        out_specs=vmem,
        out_shape=pltpu.VMEM((half.shape[0], 2 * rank), jnp.bfloat16),
        compiler_params=pltpu.CompilerParams(vmem_limit_bytes=16 * 2**20),
        cost_estimate=pl.CostEstimate(
            flops=4 * half.size * rank, bytes_accessed=2 * half.size, transcendentals=0
        ),
        name="low_values",
    )(half, down_mine, down_theirs)


def up_kernel(select, low_mine, low_theirs, up_mine, up_theirs, out):
    chips, rank, _ = up_mine.shape
    cap = select.shape[1]
    chosen = []
    for which in range(2):
        here = slice(which * rank, (which + 1) * rank)
        there = slice((1 - which) * rank, (2 - which) * rank)
        low = jnp.concatenate([low_mine[:, here], low_theirs[:, there]])
        chosen.append(jnp.dot(select[which], low, preferred_element_type=jnp.float32))
    low = jnp.concatenate(chosen, axis=1).astype(jnp.bfloat16)
    for j in range(chips):
        out[pl.ds(j * cap, cap), :] = jnp.dot(
            low,
            jnp.concatenate([up_mine[j], up_theirs[j]]),
            preferred_element_type=jnp.float32,
        ).astype(jnp.bfloat16)


def up_terms(select, low_mine, low_theirs, up_mine, up_theirs):
    cap = select.shape[1]
    chips, rank, width = up_mine.shape
    vmem = pl.BlockSpec(memory_space=pltpu.VMEM)
    return pl.pallas_call(
        up_kernel,
        in_specs=[vmem] * 5,
        out_specs=vmem,
        out_shape=jax.ShapeDtypeStruct((chips * cap, width), jnp.bfloat16),
        compiler_params=pltpu.CompilerParams(vmem_limit_bytes=16 * 2**20),
        cost_estimate=pl.CostEstimate(
            flops=4 * cap * rank * chips * width,
            bytes_accessed=2 * (2 * rank + cap) * chips * width,
            transcendentals=0,
        ),
        name="up_terms",
    )(select, low_mine, low_theirs, up_mine, up_theirs)


def chip_pool(
    normed_input_rows,
    gate_base_weight,
    adapter_down_factors,
    adapter_up_factors,
    request_adapter_id,
    row_request,
    adapter_storage_slot,
):
    npool, chips = 16, 8
    member = lax.axis_index("pool")

    def swap(value, bits):
        return lax.ppermute(value, "pool", [(i, i ^ bits) for i in range(npool)])

    far = swap(normed_input_rows, 8)
    near = swap(normed_input_rows, 4)
    side = swap(normed_input_rows, 2)
    far_near, far_diagonal = swap(far, 4), swap(far, 6)
    across = swap(jnp.concatenate([near, far]), 2)
    half = jnp.concatenate(
        [normed_input_rows, far, near, side, far_near, far_diagonal, across]
    )
    down, up = adapter_down_factors[0], adapter_up_factors[0]
    down_theirs = swap(down, 1)
    select, select_rest, pick, pick_rest, order, most, up_mine, up_swapped = prepare(
        member, request_adapter_id, row_request, adapter_storage_slot, up, chips
    )
    up_theirs = swap(up_swapped, 1)

    half, up_theirs = lax.optimization_barrier((half, up_theirs))
    low_mine = low_values(half, down, down_theirs)
    low_theirs = swap(low_mine, 1)
    terms = up_terms(select, low_mine, low_theirs, up_mine, up_theirs)
    half, terms = lax.optimization_barrier((half, terms))

    def exchange(terms):
        return lax.all_to_all(
            terms,
            "pool",
            split_axis=0,
            concat_axis=0,
            tiled=True,
            axis_index_groups=[[2 * i + c for i in range(chips)] for c in range(2)],
        )

    received = exchange(terms)
    x = jnp.concatenate([half, swap(half, 1)])
    x = jnp.dot(order, x, preferred_element_type=jnp.float32).astype(jnp.bfloat16)
    base = jnp.dot(x, gate_base_weight, preferred_element_type=jnp.float32)
    base, received = lax.optimization_barrier((base, received))

    def all_placed(base):
        return (base + jnp.dot(pick, received, preferred_element_type=jnp.float32)).astype(
            jnp.bfloat16
        )

    def some_left(base):
        up_mine, up_swapped = up_columns(member, up, chips)
        rest = exchange(
            up_terms(select_rest, low_mine, low_theirs, up_mine, swap(up_swapped, 1))
        )
        return all_placed(
            base + jnp.dot(pick_rest, rest, preferred_element_type=jnp.float32)
        )

    return lax.cond(most[0] < CHIP_CAP, all_placed, some_left, base)


def solution(mesh):
    in_specs = (
        P(("groups", "pool"), None),
        P(None, "pool"),
        P(("groups", "pool"), None, None),
        P(("groups", "pool"), None, None),
        P("groups", None),
        P("groups"),
        P("groups"),
    )
    out_specs = P("groups", "pool")

    def on_device(*blocks):
        width, share = blocks[1].shape[1], blocks[2].shape[0]
        chip_wise = mesh.shape["pool"] == 16 and width % 128 == 0 and share == 1
        return (chip_pool if chip_wise else any_pool)(*blocks)

    return jax.shard_map(
        on_device, mesh=mesh, in_specs=in_specs, out_specs=out_specs, check_vma=False
    )
```

time: 60.9 us -> 57 us (0.936)
  local copies, waits for them, and re-layouts: 3.88 us -> 0.85 us
  Pallas kernels: 8.25 us -> 5.6 us
  starting transfers between devices: 15.3 us -> 16.4 us
  other arithmetic: 0.02 us -> 0.78 us
    pallas_call x3, Pallas kernels: 8.25 us -> 5.6 us  [the longest x1 2.91 us: prepare(): pl.pallas_call(functools.partial(rows_kernel, request_adapter_id.shape[0]...]
    unnamed x13 -> x12, local copies, waits for them, and re-layouts: 3.07 us -> 0.83 us
    all_to_all x1, starting transfers between devices: 3.78 us -> 4.83 us  [exchange(): lax.all_to_all(terms, 'pool', split_axis=0, concat_axis=0, tiled=True, ax...]
    squeeze x1 -> x0, local copies, waits for them, and re-layouts: 0.79 us -> none  [row_facts(): return (select, select_rest, facts[0], facts[1], facts[2], most[0])]
    concatenate x0 -> x1, other arithmetic: none -> 0.76 us  [prepare(): jnp.concatenate([row_request, request_adapter_id[:, 0], adapter_storage_s...]
  transfers between devices with their start and end apart: 11 -> 11, of which waited for: 5 -> 5; matrix products, arithmetic and copies ran while one was open for 26% -> 24% of each run, Pallas kernels for 3% -> 5%
where the time goes in v5:
time: 57 us; the launch traced here: 56.8 us
  waiting for transfers between devices  19.5 us (34%)
  starting transfers between devices  16.4 us (29%)
  matrix products  12.9 us (23%)
  Pallas kernels  5.6 us (10%)
  local copies, waits for them, and re-layouts  0.85 us (1%)
  between operations  0.81 us (1%)
  other arithmetic  0.78 us (1%)
    dot_general x1, matrix products, chip_pool(): base = jnp.dot(x, gate_base_weight, preferred_element_type=jnp.float32)  12.6 us
    ppermute x10, starting transfers between devices, swap(): return lax.ppermute(value, 'pool', [(i, i ^ bits) for i in range(npool)])  11.5 us
    all_to_all x1, waiting for transfers between devices, exchange(): lax.all_to_all(terms, 'pool', split_axis=0, concat_axis=0, tiled=True, ax...  10.9 us
    ppermute x10, waiting for transfers between devices, swap(): return lax.ppermute(value, 'pool', [(i, i ^ bits) for i in range(npool)])  8.66 us
    all_to_all x1, starting transfers between devices, exchange(): lax.all_to_all(terms, 'pool', split_axis=0, concat_axis=0, tiled=True, ax...  4.83 us
    pallas_call x1, Pallas kernels, prepare(): pl.pallas_call(functools.partial(rows_kernel, request_adapter_id.shape[0]...  2.91 us
    pallas_call x1, Pallas kernels, up_terms(): pl.pallas_call(up_kernel, in_specs=[vmem] * 5, out_specs=vmem, out_shape=...  1.86 us
  transfers between devices with their start and end apart: 11, of which 5 were waited for; matrix products, arithmetic and copies ran while one was open for 24% of the time, Pallas kernels for 5%

profile of v5, /device:TPU:0, one launch (start us, length us, event | category | flops | bytes accessed | tf_op | source)
XLA Modules:
  0.0 56.8 jit_solution(13563264603436522717)
XLA Ops:
  0.0 4.0 %collective-permute-start.1 = (bf16[8,8192]{1,0:T(8,128)(2,1)}, bf16[8,8192]{1,0:T(8,128)(2,1)S(1)}, u32[]{:S(2)}, u32[]{:S(2)}) collective-permute-start(bf16[8,8192]{1,0:T(8,128)(2,1)} %param.9), channel_id=1, source_target_pairs={{0,8},{1,9},{2,10},{3,11},{4,12},{5,13},{6,14},{7,15},{8,0},{9,1},... | collective-permute-start | bytes 393224 | tf_op jit(solution)/shard_map/ppermute | solution.py:297
  4.0 1.6 %collective-permute-start.2 = (bf16[8,8192]{1,0:T(8,128)(2,1)}, bf16[8,8192]{1,0:T(8,128)(2,1)S(1)}, u32[]{:S(2)}, u32[]{:S(2)}) collective-permute-start(bf16[8,8192]{1,0:T(8,128)(2,1)} %param.9), channel_id=1, source_target_pairs={{0,4},{1,5},{2,6},{3,7},{4,0},{5,1},{6,2},{7,3},{8,12},{9,13},{10,... | collective-permute-start | bytes 393224 | tf_op jit(solution)/shard_map/ppermute | solution.py:297
  5.6 1.5 %collective-permute-start.3 = (bf16[8,8192]{1,0:T(8,128)(2,1)}, bf16[8,8192]{1,0:T(8,128)(2,1)S(1)}, u32[]{:S(2)}, u32[]{:S(2)}) collective-permute-start(bf16[8,8192]{1,0:T(8,128)(2,1)} %param.9), channel_id=1, source_target_pairs={{0,2},{1,3},{2,0},{3,1},{4,6},{5,7},{6,4},{7,5},{8,10},{9,11},{10,... | collective-permute-start | bytes 393224 | tf_op jit(solution)/shard_map/ppermute | solution.py:297
  7.1 0.8 %pad_add_fusion = s32[176]{0:T(256)S(1)} fusion(s32[16]{0:T(128)} %param.15, s32[32]{0:T(128)} %bitcast.30, s32[128]{0:T(128)} %param.14), kind=kLoop, calls=%fused_computation.19 | loop fusion | flops 352 | bytes 1408 | tf_op jit(solution)/shard_map/concatenate | solution.py:214
  7.9 2.9 %prepare.1 = (bf16[2,32,128]{2,1,0:T(8,128)(2,1)S(1)}, bf16[2,16,128]{2,1,0:T(8,128)(2,1)S(1)}, bf16[128,256]{1,0:T(8,128)(2,1)S(1)}, bf16[128,128]{1,0:T(8,128)...) custom-call(s32[1]{0:T(128)} %bitcast.4.member, ...), custom_call_target="tpu_custom_call" | custom-call | tf_op jit(solution)/shard_map/prepare/pallas_call | solution.py:196
  10.8 0.1 collective-permute-start.7
  10.9 0.0 copy-done
  10.9 0.5 collective-permute-start.8
  11.4 0.0 collective-permute-done.1
  11.4 0.0 collective-permute-done.2
  11.5 1.1 %collective-permute-start.6 = (bf16[16,8192]{1,0:T(8,128)(2,1)S(1)}, bf16[16,8192]{1,0:T(8,128)(2,1)S(1)}, u32[]{:S(2)}, u32[]{:S(2)}) collective-permute-start(bf16[16,8192]{1,0:T(8,128)(2,1)S(1)} %pad_maximum_fusion), channel_id=1, source_target_pairs={{0,2},{1,3},{2,0},{3,1},{4,6},{5,7},{6,4},{7,5},{8,10},{9,11},{10,... | collective-permute-start | bytes 786440 | tf_op jit(solution)/shard_map/ppermute | solution.py:297
  12.5 1.4 %collective-permute-start.4 = (bf16[8,8192]{1,0:T(8,128)(2,1)S(1)}, bf16[8,8192]{1,0:T(8,128)(2,1)S(1)}, u32[]{:S(2)}, u32[]{:S(2)}) collective-permute-start(bf16[8,8192]{1,0:T(8,128)(2,1)S(1)} %collective-permute-done.1), channel_id=1, source_target_pairs={{0,4},{1,5},{2,6},{3,7},{4,0},{5,1},{6,2},{7,3},{8,12},{9,13},{10,... | collective-permute-start | bytes 393224 | tf_op jit(solution)/shard_map/ppermute | solution.py:297
  13.9 0.0 collective-permute-done.3
  14.0 1.2 %collective-permute-start.5 = (bf16[8,8192]{1,0:T(8,128)(2,1)S(1)}, bf16[8,8192]{1,0:T(8,128)(2,1)S(1)}, u32[]{:S(2)}, u32[]{:S(2)}) collective-permute-start(bf16[8,8192]{1,0:T(8,128)(2,1)S(1)} %collective-permute-done.1), channel_id=1, source_target_pairs={{0,6},{1,7},{2,4},{3,5},{4,2},{5,3},{6,0},{7,1},{8,14},{9,15},{10,... | collective-permute-start | bytes 393224 | tf_op jit(solution)/shard_map/ppermute | solution.py:297
  15.1 3.5 %collective-permute-done.4 = bf16[8,8192]{1,0:T(8,128)(2,1)S(1)} collective-permute-done((bf16[8,8192]{1,0:T(8,128)(2,1)S(1)}, bf16[8,8192]{1,0:T(8,128)(2,1)S(1)}, u32[]{:S(2)}, u32[]{:S(2)}) %collective-permute-start.4) | collective-permute-done | bytes 131104 | tf_op jit(solution)/shard_map/ppermute | solution.py:297
  18.7 2.5 %collective-permute-done.5 = bf16[8,8192]{1,0:T(8,128)(2,1)S(1)} collective-permute-done((bf16[8,8192]{1,0:T(8,128)(2,1)S(1)}, bf16[8,8192]{1,0:T(8,128)(2,1)S(1)}, u32[]{:S(2)}, u32[]{:S(2)}) %collective-permute-start.5) | collective-permute-done | bytes 131104 | tf_op jit(solution)/shard_map/ppermute | solution.py:297
  21.1 1.5 %collective-permute-done.6 = bf16[16,8192]{1,0:T(8,128)(2,1)S(1)} collective-permute-done((bf16[16,8192]{1,0:T(8,128)(2,1)S(1)}, bf16[16,8192]{1,0:T(8,128)(2,1)S(1)}, u32[]{:S(2)}, u32[]{:S(2)}) %collective-permute-start.6) | collective-permute-done | bytes 262176 | tf_op jit(solution)/shard_map/ppermute | solution.py:297
  22.7 0.0 collective-permute-done.7.up_theirs
  22.7 0.0 collective-permute-done.8.down_theirs
  22.7 0.8 %low_values.1.low_mine = bf16[64,128]{1,0:T(8,128)(2,1)S(1)} custom-call(bf16[64,8192]{1,0:T(8,128)(2,1)S(1)} %constant_dynamic-update-slice_fusion.half, bf16[64,8192]{1,0:T(8,128)(2,1)S(1)} %bitcast.24, bf16[64,8192]{1,0:T(8,128)(2,1)S(1)} %collective-permute-done.8.down_theirs), custom_call_target="tpu_custom_call" | custom-call | flops 134217728 | bytes 1048576 | tf_op jit(solution)/shard_map/low_values/pallas_call | solution.py:234
  23.5 0.1 collective-permute-start.9
  23.6 1.2 %collective-permute-done.9.low_theirs = bf16[64,128]{1,0:T(8,128)(2,1)S(1)} collective-permute-done((bf16[64,128]{1,0:T(8,128)(2,1)S(1)}, bf16[64,128]{1,0:T(8,128)(2,1)S(1)}, u32[]{:S(2)}, u32[]{:S(2)}) %collective-permute-start.9) | collective-permute-done | bytes 16416 | tf_op jit(solution)/shard_map/ppermute | solution.py:297
  24.8 1.9 %up_terms.3 = bf16[256,1792]{1,0:T(8,128)(2,1)} custom-call(bf16[2,32,128]{2,1,0:T(8,128)(2,1)S(1)} %get-tuple-element.72.select, bf16[64,128]{1,0:T(8,128)(2,1)S(1)} %low_values.1.low_mine, bf16[64,128]{1,0:T(8,128)(2,1)S(1)} %collective-permute-done.9.low_theirs, bf16[8,64,1792]{2,1,0:T(8,128)(2,1)S(1)} %get-tuple-element.73.up_mine, ...), custom_call_target="tpu_custom_call" | custom-call | flops 117440512 | bytes 4587520 | tf_op jit(solution)/shard_map/up_terms/pallas_call | solution.py:269
  26.6 0.2 collective-permute-start.10
  27.4 4.8 %all-to-all-start.1 = ((bf16[8,32,1792]{2,1,0:T(8,128)(2,1)}), bf16[8,32,1792]{2,1,0:T(8,128)(2,1)S(1)}, u32[]{:S(2)}, u32[]{:S(2)}) async-start(bf16[8,32,1792]{2,1,0:T(8,128)(2,1)} %bitcast.10), calls=%async_computation.1 | async-start | bytes 1835008 | tf_op jit(solution)/shard_map/all_to_all | solution.py:321
  32.3 0.0 collective-permute-done.10
  32.3 12.6 %fusion.7 = f32[128,1792]{1,0:T(8,128)S(1)} fusion(bf16[8192,1792]{1,0:T(8,128)(2,1)} %param.10, bf16[128,128]{1,0:T(8,128)(2,1)S(1)} %get-tuple-element.71, bf16[64,8192]{1,0:T(8,128)(2,1)} %collective-permute-done.10, bf16[64,8192]{1,0:T(8,128)(2,1)S(1)} %constant_dynamic-update-slice_fusion.half), kind=kOutput, calls=%fused_computation.10 | convolution fusion | flops 4031774720 | bytes 32407552 | tf_op jit(solution)/shard_map/dot_general | solution.py:333
  44.9 10.9 %all-to-all-done.1 = bf16[8,32,1792]{2,1,0:T(8,128)(2,1)S(1)} async-done(((bf16[8,32,1792]{2,1,0:T(8,128)(2,1)}), bf16[8,32,1792]{2,1,0:T(8,128)(2,1)S(1)}, u32[]{:S(2)}, u32[]{:S(2)}) %all-to-all-start.1) | async-done | bytes 917536 | tf_op jit(solution)/shard_map/all_to_all | solution.py:321
  55.8 0.3 conditional.6
  55.8 0.3 fusion.2
  56.1 0.0 copy-start.1
  56.1 0.8 %copy-done.1 = bf16[128,1792]{1,0:T(8,128)(2,1)} copy-done((bf16[128,1792]{1,0:T(8,128)(2,1)}, bf16[128,1792]{1,0:T(8,128)(2,1)S(1)}, u32[]{:S(2)}) %copy-start.1) | copy-done | bytes 458776
  (11 shorter events, 0.1 us)
Async XLA Ops:
  0.0 11.4 %copy-start.2 = (bf16[8,8192]{1,0:T(8,128)(2,1)S(1)}, bf16[8,8192]{1,0:T(8,128)(2,1)}, u32[]{:S(2)}) copy-start(bf16[8,8192]{1,0:T(8,128)(2,1)} %param.9) | copy-start | bytes 393220
  0.0 10.9 %copy-start = (bf16[1,64,8192]{2,1,0:T(8,128)(2,1)S(1)}, bf16[1,64,8192]{2,1,0:T(8,128)(2,1)}, u32[]{:S(2)}) copy-start(bf16[1,64,8192]{2,1,0:T(8,128)(2,1)} %param.11) | copy-start | bytes 3145732
  0.0 11.4 %collective-permute-start.1 = (bf16[8,8192]{1,0:T(8,128)(2,1)}, bf16[8,8192]{1,0:T(8,128)(2,1)S(1)}, u32[]{:S(2)}, u32[]{:S(2)}) collective-permute-start(bf16[8,8192]{1,0:T(8,128)(2,1)} %param.9), channel_id=1, source_target_pairs={{0,8},{1,9},{2,10},{3,11},{4,12},{5,13},{6,14},{7,15},{8,0},{9,1},... | collective-permute-start | bytes 393224 | tf_op jit(solution)/shard_map/ppermute | solution.py:297
  4.0 7.4 %collective-permute-start.2 = (bf16[8,8192]{1,0:T(8,128)(2,1)}, bf16[8,8192]{1,0:T(8,128)(2,1)S(1)}, u32[]{:S(2)}, u32[]{:S(2)}) collective-permute-start(bf16[8,8192]{1,0:T(8,128)(2,1)} %param.9), channel_id=1, source_target_pairs={{0,4},{1,5},{2,6},{3,7},{4,0},{5,1},{6,2},{7,3},{8,12},{9,13},{10,... | collective-permute-start | bytes 393224 | tf_op jit(solution)/shard_map/ppermute | solution.py:297
  5.6 8.3 %collective-permute-start.3 = (bf16[8,8192]{1,0:T(8,128)(2,1)}, bf16[8,8192]{1,0:T(8,128)(2,1)S(1)}, u32[]{:S(2)}, u32[]{:S(2)}) collective-permute-start(bf16[8,8192]{1,0:T(8,128)(2,1)} %param.9), channel_id=1, source_target_pairs={{0,2},{1,3},{2,0},{3,1},{4,6},{5,7},{6,4},{7,5},{8,10},{9,11},{10,... | collective-permute-start | bytes 393224 | tf_op jit(solution)/shard_map/ppermute | solution.py:297
  10.8 11.8 %collective-permute-start.7 = (bf16[8,64,1792]{2,1,0:T(8,128)(2,1)S(1)}, bf16[8,64,1792]{2,1,0:T(8,128)(2,1)S(1)}, u32[]{:S(2)}, u32[]{:S(2)}) collective-permute-start(bf16[8,64,1792]{2,1,0:T(8,128)(2,1)S(1)} %get-tuple-element.68), channel_id=1, source_target_pairs={{0,1},{1,0},{2,3},{3,2},{4,5},{5,4},{6,7},{7,6},{8,9},{9,8},{10,11... | collective-permute-start | bytes 5505032 | tf_op jit(solution)/shard_map/ppermute | solution.py:297
  10.9 11.8 %collective-permute-start.8 = (bf16[64,8192]{1,0:T(8,128)(2,1)S(1)}, bf16[64,8192]{1,0:T(8,128)(2,1)S(1)}, u32[]{:S(2)}, u32[]{:S(2)}) collective-permute-start(bf16[64,8192]{1,0:T(8,128)(2,1)S(1)} %bitcast.23), channel_id=1, source_target_pairs={{0,1},{1,0},{2,3},{3,2},{4,5},{5,4},{6,7},{7,6},{8,9},{9,8},{10,11... | collective-permute-start | bytes 3145736 | tf_op jit(solution)/shard_map/ppermute | solution.py:297
  11.5 11.2 %collective-permute-start.6 = (bf16[16,8192]{1,0:T(8,128)(2,1)S(1)}, bf16[16,8192]{1,0:T(8,128)(2,1)S(1)}, u32[]{:S(2)}, u32[]{:S(2)}) collective-permute-start(bf16[16,8192]{1,0:T(8,128)(2,1)S(1)} %pad_maximum_fusion), channel_id=1, source_target_pairs={{0,2},{1,3},{2,0},{3,1},{4,6},{5,7},{6,4},{7,5},{8,10},{9,11},{10,... | collective-permute-start | bytes 786440 | tf_op jit(solution)/shard_map/ppermute | solution.py:297
  12.5 6.1 %collective-permute-start.4 = (bf16[8,8192]{1,0:T(8,128)(2,1)S(1)}, bf16[8,8192]{1,0:T(8,128)(2,1)S(1)}, u32[]{:S(2)}, u32[]{:S(2)}) collective-permute-start(bf16[8,8192]{1,0:T(8,128)(2,1)S(1)} %collective-permute-done.1), channel_id=1, source_target_pairs={{0,4},{1,5},{2,6},{3,7},{4,0},{5,1},{6,2},{7,3},{8,12},{9,13},{10,... | collective-permute-start | bytes 393224 | tf_op jit(solution)/shard_map/ppermute | solution.py:297
  14.0 7.2 %collective-permute-start.5 = (bf16[8,8192]{1,0:T(8,128)(2,1)S(1)}, bf16[8,8192]{1,0:T(8,128)(2,1)S(1)}, u32[]{:S(2)}, u32[]{:S(2)}) collective-permute-start(bf16[8,8192]{1,0:T(8,128)(2,1)S(1)} %collective-permute-done.1), channel_id=1, source_target_pairs={{0,6},{1,7},{2,4},{3,5},{4,2},{5,3},{6,0},{7,1},{8,14},{9,15},{10,... | collective-permute-start | bytes 393224 | tf_op jit(solution)/shard_map/ppermute | solution.py:297
  23.5 1.2 %collective-permute-start.9 = (bf16[64,128]{1,0:T(8,128)(2,1)S(1)}, bf16[64,128]{1,0:T(8,128)(2,1)S(1)}, u32[]{:S(2)}, u32[]{:S(2)}) collective-permute-start(bf16[64,128]{1,0:T(8,128)(2,1)S(1)} %low_values.1.low_mine), channel_id=1, source_target_pairs={{0,1},{1,0},{2,3},{3,2},{4,5},{5,4},{6,7},{7,6},{8,9},{9,8},{10,11... | collective-permute-start | bytes 49160 | tf_op jit(solution)/shard_map/ppermute | solution.py:297
  26.6 5.7 %collective-permute-start.10 = (bf16[64,8192]{1,0:T(8,128)(2,1)S(1)}, bf16[64,8192]{1,0:T(8,128)(2,1)}, u32[]{:S(2)}, u32[]{:S(2)}) collective-permute-start(bf16[64,8192]{1,0:T(8,128)(2,1)S(1)} %constant_dynamic-update-slice_fusion.half), channel_id=1, source_target_pairs={{0,1},{1,0},{2,3},{3,2},{4,5},{5,4},{6,7},{7,6},{8,9},{9,8},{10,11... | collective-permute-start | bytes 3145736 | tf_op jit(solution)/shard_map/ppermute | solution.py:297
  27.4 28.3 %all-to-all-start.1 = ((bf16[8,32,1792]{2,1,0:T(8,128)(2,1)}), bf16[8,32,1792]{2,1,0:T(8,128)(2,1)S(1)}, u32[]{:S(2)}, u32[]{:S(2)}) async-start(bf16[8,32,1792]{2,1,0:T(8,128)(2,1)} %bitcast.10), calls=%async_computation.1 | async-start | bytes 1835008 | tf_op jit(solution)/shard_map/all_to_all | solution.py:321
  56.1 0.8 %copy-start.1 = (bf16[128,1792]{1,0:T(8,128)(2,1)}, bf16[128,1792]{1,0:T(8,128)(2,1)S(1)}, u32[]{:S(2)}) copy-start(bf16[128,1792]{1,0:T(8,128)(2,1)S(1)} %get-tuple-element.107) | copy-start | bytes 1376260
